TPU v7x, 1024 devices: a whole 4x4x32 slice. The times are simulated.
1024 devices in a mesh: dom: 16 (over y, x), grp: 64 (over z, core).
Axes of the slice: x: 4, y: 4, z: 32, core: 2. Of those that a mesh axis runs over, the one named last changes fastest.
Arguments:
- features: bfloat16 [262144, 256], P(('dom', 'grp')), may hold values from -6 to 6
- adjacency: bfloat16 [16384, 128, 128], P(('dom', 'grp')), may hold values from -0.1875 to 0.1875
- src_tile: int32 [16384], P(('dom', 'grp')), may hold values from 0 to 1
- dst_peer: int32 [16384, 1], P(('dom', 'grp')), may hold values from 0 to 15; in each aligned block of 16 rows (0 to 15, 16 to 31, ...) at most 2 rows name the same one
- dst_tile: int32 [16384], P(('dom', 'grp')), may hold values from 0 to 1
- w_self: bfloat16 [256, 256], replicated, may hold values from -0.375 to 0.375
- w_neigh: bfloat16 [256, 256], replicated, may hold values from -0.375 to 0.375
- out_grad: bfloat16 [262144, 256], P(('dom', 'grp')), may hold values from -6 to 6
Outputs:
- output: bfloat16 [262144, 256], P(('dom', 'grp'))
- feat_grad: bfloat16 [262144, 256], P(('dom', 'grp'))
- weight_grads: float32 [2, 256, 256], replicated
Inputs may be any that keep to these rules, and one draw needn't show every extreme that they name: `dst_peer`: among the 16 blocks of one device no partition is named more than 2 times, a bound that some block reaches.
All inputs are finite; a program needn't handle non-finite values.
Results may differ from a plain program's by a relative error of at most 0.015.
Values may be sent and summed in bfloat16 or wider, within the bound.
No kernel may reach another device: no remote copies, remote signals or barrier semaphores. Data moves between devices by JAX's collectives and lax.ppermute only.
A program may use at most 32 MiB of HBM per device.

v0:
```python
import math

import jax
import jax.numpy as jnp
from jax import lax
from jax.sharding import PartitionSpec as P


def body(features, adjacency, src_tile, dst_peer, dst_tile, w_self, w_neigh, out_grad):
    nodes, width = features.shape
    tile = adjacency.shape[1]
    n_tiles = nodes // tile
    parts = lax.axis_size("dom")
    blocks = features.reshape(n_tiles, tile, width)
    products = jnp.einsum(
        "tij,tjf->tif", adjacency, blocks[src_tile], preferred_element_type=jnp.float32
    ).astype(jnp.bfloat16)
    peers = dst_peer[:, 0]
    target = peers * n_tiles + dst_tile
    dense = (
        jnp.zeros((parts * n_tiles, tile, width), jnp.float32)
        .at[target]
        .add(products.astype(jnp.float32))
    )
    flat = dense.reshape(parts * nodes, width)
    agg = lax.psum_scatter(flat, "dom", scatter_dimension=0, tiled=True)
    agg_low = agg.astype(jnp.bfloat16)
    pre = jnp.dot(features, w_self, preferred_element_type=jnp.float32) + jnp.dot(
        agg_low, w_neigh, preferred_element_type=jnp.float32
    )
    sig = jax.nn.sigmoid(pre)
    output = (pre * sig).astype(jnp.bfloat16)
    dpre = (out_grad.astype(jnp.float32) * sig * (1.0 + pre * (1.0 - sig))).astype(jnp.bfloat16)
    total_nodes = nodes * parts * lax.axis_size("grp")
    scale = 1.0 / math.sqrt(total_nodes)
    contract = (((0,), (0,)), ((), ()))
    grad_self = lax.dot_general(features, dpre, contract, preferred_element_type=jnp.float32)
    grad_neigh = lax.dot_general(agg_low, dpre, contract, preferred_element_type=jnp.float32)
    agg_grad = jnp.dot(dpre, w_neigh.T, preferred_element_type=jnp.float32).astype(jnp.bfloat16)
    everyone = lax.all_gather(agg_grad, "dom", axis=0, tiled=True).reshape(
        parts * n_tiles, tile, width
    )
    picked = everyone[peers * n_tiles + dst_tile]
    back = jnp.einsum("tij,tif->tjf", adjacency, picked, preferred_element_type=jnp.float32)
    spread = (
        jnp.zeros((n_tiles, tile, width), jnp.float32).at[src_tile].add(back).reshape(nodes, width)
    )
    feat_grad = (jnp.dot(dpre, w_self.T, preferred_element_type=jnp.float32) + spread).astype(
        jnp.bfloat16
    )
    total_self, total_neigh = lax.psum((grad_self, grad_neigh), ("dom", "grp"))
    weight_grads = jnp.stack([total_self * scale, total_neigh * scale])
    return (output, feat_grad, weight_grads)


def solution(mesh):
    in_specs = (
        P(("dom", "grp"), None),
        P(("dom", "grp"), None, None),
        P(("dom", "grp")),
        P(("dom", "grp"), None),
        P(("dom", "grp")),
        P(),
        P(),
        P(("dom", "grp"), None),
    )
    out_specs = (P(("dom", "grp"), None), P(("dom", "grp"), None), P())
    return jax.shard_map(body, mesh=mesh, in_specs=in_specs, out_specs=out_specs, check_vma=False)
```

profile of v0, /device:TPU:1, one launch (start us, length us, event | category | flops | bytes accessed | tf_op | source)
XLA Modules:
  0.0 1129.7 jit_solution(18014094361450779592)
XLA Ops:
  7.2 0.0 copy-start
  7.2 0.0 reduce-scatter.2.cloned.1.call-start
  7.2 0.7 compare_select_fusion
  7.9 1.5 gather_fusion
  9.5 0.0 copy-done
  9.5 1.8 convert_bitcast_fusion
  11.3 0.0 copy-start.6
  11.3 0.0 copy-start.7
  11.3 1.9 copy.16
  13.3 0.0 copy-done.6
  13.3 0.0 copy-done.7
  13.3 2.4 broadcast_in_dim.14
  15.7 4.6 scatter_fusion
  20.3 0.0 copy-start.1
  20.3 0.0 copy-start.2
  20.3 0.0 copy-start.4
  20.3 0.0 copy-start.5
  20.3 0.0 reduce-scatter.2.cloned.1.call-update
  20.3 0.0 all-reduce.3.cloned.1.call-start
  20.4 0.8 copy-done.1
  21.2 0.1 copy-done.2
  21.3 0.2 fusion.4
  21.4 119.2 %reduce-scatter.2.cloned.1.call-done = f32[256,256]{1,0:T(8,128)} async-done(((f32[4096,256]{1,0:T(8,128)}), f32[256,256]{1,0:T(8,128)}) %reduce-scatter.2.cloned.1.call-update) | async-done | bytes 262160 | tf_op jit(solution)/shard_map/reduce_scatter | solution.py:26
  140.6 0.0 copy-done.4
  140.6 0.0 copy-done.5
  140.6 0.0 copy-start.3
  140.6 2.0 multiply_convert_fusion
  142.6 0.9 convolution_bitcast_fusion.1
  143.5 0.0 copy-done.3
  143.5 0.9 fusion.1
  144.5 0.0 all-reduce.3.cloned.1.call-update
  144.5 0.0 all-gather.2.cloned.1.call-start
  144.5 0.9 convolution_convert_fusion.1
  145.4 0.0 all-gather.2.cloned.1.call-update
  145.5 890.1 %all-reduce.3.cloned.1.call-done = (f32[256,256]{0,1:T(8,128)}, f32[256,256]{0,1:T(8,128)}) async-done(((f32[256,256]{0,1:T(8,128)}, f32[256,256]{0,1:T(8,128)}), (f32[256,256]{0,1:T(8,128)}, f32[256,256]{0,1:T(8,128)})) %all-reduce.3.cloned.1.call-update) | async-done | bytes 524304 | tf_op jit(solution)/shard_map/psum | solution.py:51
  1035.5 1.1 multiply_bitcast_fusion
  1036.6 1.0 copy.20
  1037.6 76.5 %all-gather.2.cloned.1.call-done = bf16[4096,256]{1,0:T(8,128)(2,1)} async-done(((bf16[256,256]{1,0:T(8,128)(2,1)}), bf16[4096,256]{1,0:T(8,128)(2,1)}) %all-gather.2.cloned.1.call-update) | async-done | bytes 2097168 | tf_op jit(solution)/shard_map/all_gather | solution.py:40
  1114.1 2.2 gather_fusion.1
  1116.3 1.8 convolution_bitcast_fusion
  1118.2 1.9 copy.18
  1120.1 2.2 scatter_fusion.1
  1122.3 0.9 fusion
  (5 shorter events, 0.1 us)
Async XLA Ops:
  7.2 2.3 copy-start
  7.2 133.5 %reduce-scatter.2.cloned.1.call-start = ((), (), s32[]{:S(2)}) async-start(), calls=%async_computation.1 | async-start | bytes 4456448 | tf_op jit(solution)/shard_map/reduce_scatter | solution.py:26
  11.3 2.0 copy-start.6
  11.3 2.0 copy-start.7
  20.3 0.9 copy-start.1
  20.3 1.0 copy-start.2
  20.3 120.3 %copy-start.4 = (bf16[256,256]{1,0:T(8,128)(2,1)S(1)}, bf16[256,256]{1,0:T(8,128)(2,1)}, u32[]{:S(2)}) copy-start(bf16[256,256]{1,0:T(8,128)(2,1)} %param.14) | copy-start | bytes 393220
  20.3 120.3 %copy-start.5 = (bf16[256,256]{1,0:T(8,128)(2,1)S(1)}, bf16[256,256]{1,0:T(8,128)(2,1)}, u32[]{:S(2)}) copy-start(bf16[256,256]{1,0:T(8,128)(2,1)} %param.15) | copy-start | bytes 393220
  20.3 1015.2 %all-reduce.3.cloned.1.call-start = ((), (), s32[]{:S(2)}) async-start(), calls=%async_computation.3 | async-start | bytes 1048576 | tf_op jit(solution)/shard_map/psum | solution.py:51
  140.6 2.9 copy-start.3
  144.5 969.6 %all-gather.2.cloned.1.call-start = ((), (), s32[]{:S(2)}) async-start(), calls=%async_computation.2 | async-start | bytes 2228224 | tf_op jit(solution)/shard_map/all_gather | solution.py:40
Sparse Core Ops, SparseCore 0:
  20.4 120.1 reduce-scatter.1
  147.6 887.8 all-reduce.2
  1040.3 73.8 all-gather.1
where the time goes:
time: 1130 us
  waiting for transfers between devices  1090 us (96%)
  between operations  13.9 us (1%)
  local copies, waits for them, and re-layouts  11.9 us (1%)
    psum x1, waiting for transfers between devices, body(): total_self, total_neigh = lax.psum((grad_self, grad_neigh), ('dom', 'grp'))  890 us
    reduce_scatter x1, waiting for transfers between devices, body(): agg = lax.psum_scatter(flat, 'dom', scatter_dimension=0, tiled=True)  119 us
    all_gather x1, waiting for transfers between devices, body(): lax.all_gather(agg_grad, 'dom', axis=0, tiled=True)  76.5 us
  transfers between devices with their start and end apart: 3, of which 3 were waited for; matrix products, arithmetic and copies ran while one was open for 0% of the time, Pallas kernels for 0%

commit v1 on v0

v1 whole, which is shorter than its diff:
```python
import math

import jax
import jax.numpy as jnp
from jax import lax
from jax.experimental import pallas as pl
from jax.experimental.pallas import tpu as pltpu
from jax.sharding import Mesh
from jax.sharding import PartitionSpec as P

F32 = jnp.float32
BF16 = jnp.bfloat16
Z_LO = 2
LINE = ("y", "x")
NEAR = ("y", "x", "z_lo", "core")
FAR = "z_hi"
ALL = ("y", "x", "z_hi", "z_lo", "core")
TN = (((0,), (0,)), ((), ()))
NT = (((1,), (1,)), ((), ()))
LIMIT = 32 * 1024 * 1024


def smem():
    return pl.BlockSpec(memory_space=pltpu.SMEM)


def vmem():
    return pl.BlockSpec(memory_space=pltpu.VMEM)


def call(kernel, outs, n_smem, n_vmem, scratch=(), flops=0, size=0):
    return pl.pallas_call(
        kernel,
        out_shape=outs,
        in_specs=[smem()] * n_smem + [vmem()] * n_vmem,
        out_specs=jax.tree.map(lambda _: vmem(), outs),
        scratch_shapes=list(scratch),
        compiler_params=pltpu.CompilerParams(vmem_limit_bytes=LIMIT),
        cost_estimate=pl.CostEstimate(flops=flops, bytes_accessed=size, transcendentals=0),
    )


def shape(dims, dtype):
    return jax.ShapeDtypeStruct(dims, dtype)


def partial_sums(src_ref, peer_ref, dst_ref, feat_ref, adj_ref, out_ref):
    count, tile, _ = adj_ref.shape
    out_ref[...] = jnp.zeros_like(out_ref)
    for t in range(count):
        src = pl.multiple_of(src_ref[t] * tile, tile)
        dst = pl.multiple_of(dst_ref[t] * tile, tile)
        prod = jnp.dot(adj_ref[t], feat_ref[pl.ds(src, tile), :], preferred_element_type=F32)
        where = (peer_ref[t, 0], pl.ds(dst, tile), slice(None))
        out_ref[where] = (out_ref[where].astype(F32) + prod.astype(BF16).astype(F32)).astype(BF16)


def layer(recv_ref, feat_ref, ws_ref, wn_ref, grad_ref, out_ref, base_ref, agg_grad_ref, wg_ref):
    peers, nodes, width = recv_ref.shape
    agg = recv_ref[0].astype(F32)
    for p in range(1, peers):
        agg = agg + recv_ref[p].astype(F32)
    low = agg.astype(BF16)
    feat = feat_ref[...]
    pre = jnp.dot(feat, ws_ref[...], preferred_element_type=F32) + jnp.dot(
        low, wn_ref[...], preferred_element_type=F32
    )
    sig = jax.nn.sigmoid(pre)
    out_ref[...] = (pre * sig).astype(BF16)
    dpre = (grad_ref[...].astype(F32) * sig * (1.0 + pre * (1.0 - sig))).astype(BF16)
    chunks, rows, lanes = wg_ref.shape
    half = chunks // 2
    for k, left in enumerate((feat, low)):
        part = lax.dot_general(left, dpre, TN, preferred_element_type=F32)
        part = part.reshape(half, rows // 2, width)
        part = jnp.concatenate([part[:, :, :lanes], part[:, :, lanes:]], axis=1)
        wg_ref[k * half : (k + 1) * half] = part.astype(BF16)
    agg_grad = lax.dot_general(dpre, wn_ref[...], NT, preferred_element_type=F32).astype(BF16)
    for p in range(peers):
        agg_grad_ref[p] = agg_grad
    base_ref[...] = lax.dot_general(dpre, ws_ref[...], NT, preferred_element_type=F32)


def gradient(src_ref, peer_ref, dst_ref, adj_ref, every_ref, base_ref, out_ref, acc_ref):
    count, tile, _ = adj_ref.shape
    acc_ref[...] = base_ref[...]
    for t in range(count):
        src = pl.multiple_of(src_ref[t] * tile, tile)
        dst = pl.multiple_of(dst_ref[t] * tile, tile)
        picked = every_ref[peer_ref[t, 0], pl.ds(dst, tile), :]
        acc_ref[pl.ds(src, tile), :] += lax.dot_general(
            adj_ref[t], picked, TN, preferred_element_type=F32
        )
    out_ref[...] = acc_ref[...].astype(BF16)


def spread_sum(in_ref, out_ref):
    total = jnp.sum(in_ref[...].astype(F32), axis=0).astype(out_ref.dtype)
    for p in range(out_ref.shape[0]):
        out_ref[p] = total


def unpack(in_ref, out_ref, *, scale):
    got = in_ref[...].astype(F32) * scale
    chunks, rows, lanes = got.shape
    got = jnp.concatenate([got[:, : rows // 2], got[:, rows // 2 :]], axis=2)
    out_ref[...] = got.reshape(out_ref.shape)


def body(features, adjacency, src_tile, dst_peer, dst_tile, w_self, w_neigh, out_grad):
    nodes, width = features.shape
    count, tile, _ = adjacency.shape
    parts = lax.axis_size(LINE)
    near, far = lax.axis_size(NEAR), lax.axis_size(FAR)
    total_nodes = nodes * lax.axis_size(ALL)
    rows = 2 * width * width // near // 128
    dense = call(
        partial_sums,
        shape((parts, nodes, width), BF16),
        3,
        2,
        flops=2 * count * tile * tile * width,
        size=3 << 20,
    )(src_tile, dst_peer, dst_tile, features, adjacency)
    recv = lax.all_to_all(dense, LINE, 0, 0)
    output, base, mine, wgrad = call(
        layer,
        (
            shape((nodes, width), BF16),
            shape((nodes, width), F32),
            shape((parts, nodes, width), BF16),
            shape((near, rows, 128), BF16),
        ),
        0,
        5,
        flops=12 * nodes * width * width,
        size=5 << 20,
    )(recv, features, w_self, w_neigh, out_grad)
    wgrad = lax.all_to_all(wgrad, NEAR, 0, 0)
    wgrad = call(spread_sum, shape((far, rows, 128), BF16), 0, 1, size=1 << 19)(wgrad)
    every = lax.all_to_all(mine, LINE, 0, 0)
    wgrad = lax.all_to_all(wgrad, FAR, 0, 0)
    wgrad = call(spread_sum, shape((near, rows, 128), BF16), 0, 1, size=1 << 19)(wgrad)
    wgrad = lax.all_to_all(wgrad, NEAR, 0, 0)
    feat_grad = call(
        gradient,
        shape((nodes, width), BF16),
        3,
        3,
        scratch=[pltpu.VMEM((nodes, width), F32)],
        flops=2 * count * tile * tile * width,
        size=3 << 20,
    )(src_tile, dst_peer, dst_tile, adjacency, every, base)

    def last(in_ref, out_ref):
        unpack(in_ref, out_ref, scale=1.0 / math.sqrt(total_nodes))

    weight_grads = call(last, shape((2, width, width), F32), 0, 1, size=1 << 20)(wgrad)
    return (output, feat_grad, weight_grads)


def solution(mesh):
    dom, grp = mesh.devices.shape
    side = math.isqrt(dom)
    fine = Mesh(
        mesh.devices.reshape(side, dom // side, grp // (2 * Z_LO), Z_LO, 2), ALL
    )
    rows = P(ALL, None)
    in_specs = (rows, P(ALL, None, None), P(ALL), rows, P(ALL), P(), P(), rows)
    out_specs = (rows, rows, P())
    return jax.shard_map(body, mesh=fine, in_specs=in_specs, out_specs=out_specs, check_vma=False)
```

time: 1130 us -> 159 us (0.14)
  waiting for transfers between devices: 1090 us -> 32.8 us
  blocking collectives: 0 us -> 100 us
  starting transfers between devices: 0.12 us -> 13.6 us
  between operations: 13.9 us -> 0.73 us
    psum x1 -> x0, waiting for transfers between devices: 890 us -> none  [body(): total_self, total_neigh = lax.psum((grad_self, grad_neigh), ('dom', 'grp'))]
    reduce_scatter x1 -> x0, waiting for transfers between devices: 119 us -> none  [body(): agg = lax.psum_scatter(flat, 'dom', scatter_dimension=0, tiled=True)]
    all_to_all x0 -> x3, blocking collectives: none -> 100 us  [the longest x1 48.6 us: body(): wgrad = lax.all_to_all(wgrad, FAR, 0, 0)]
    all_gather x1 -> x0, waiting for transfers between devices: 76.5 us -> none  [body(): lax.all_gather(agg_grad, 'dom', axis=0, tiled=True)]
    all_to_all x0 -> x2, waiting for transfers between devices: none -> 32.8 us  [the longest x1 24.5 us: body(): every = lax.all_to_all(mine, LINE, 0, 0)]
    all_to_all x0 -> x2, starting transfers between devices: none -> 13.6 us  [the longest x1 9.8 us: body(): wgrad = lax.all_to_all(wgrad, NEAR, 0, 0)]
  transfers between devices with their start and end apart: 3 -> 2, of which waited for: 3 -> 2; matrix products, arithmetic and copies ran while one was open for 0% -> 0% of each run, Pallas kernels for 0% -> 2%
where the time goes in v1:
time: 159 us
  blocking collectives  100 us (63%)
  waiting for transfers between devices  32.8 us (21%)
  starting transfers between devices  13.6 us (9%)
  Pallas kernels  5.86 us (4%)
  local copies, waits for them, and re-layouts  5.35 us (3%)
    all_to_all x1, blocking collectives, body(): wgrad = lax.all_to_all(wgrad, FAR, 0, 0)  48.6 us
    all_to_all x1, blocking collectives, body(): recv = lax.all_to_all(dense, LINE, 0, 0)  26.6 us
    all_to_all x1, blocking collectives, body(): wgrad = lax.all_to_all(wgrad, NEAR, 0, 0)  25 us
    all_to_all x1, waiting for transfers between devices, body(): every = lax.all_to_all(mine, LINE, 0, 0)  24.5 us
    all_to_all x1, starting transfers between devices, body(): wgrad = lax.all_to_all(wgrad, NEAR, 0, 0)  9.8 us
    all_to_all x1, waiting for transfers between devices, body(): wgrad = lax.all_to_all(wgrad, NEAR, 0, 0)  8.25 us
    unnamed x25, local copies, waits for them, and re-layouts  5.35 us
    all_to_all x1, starting transfers between devices, body(): every = lax.all_to_all(mine, LINE, 0, 0)  3.85 us
  transfers between devices with their start and end apart: 2, of which 2 were waited for; matrix products, arithmetic and copies ran while one was open for 0% of the time, Pallas kernels for 2%

profile of v1, /device:TPU:1, one launch (start us, length us, event | category | flops | bytes accessed | tf_op | source)
XLA Modules:
  0.0 158.5 jit_solution(14632304370505916388)
XLA Ops:
  0.6 0.7 copy.11.peer_ref
  1.4 0.0 copy-start.1
  1.4 1.0 copy-done.1
  2.4 0.0 copy-start.3
  2.4 0.9 copy-done.3
  3.3 0.0 copy-start.8
  3.3 0.7 copy-done.8
  4.0 0.0 copy-start.10
  4.0 0.7 copy-done.10
  4.6 1.2 shard_map.103
  5.9 0.0 copy-start.4
  5.9 0.0 copy-start.5
  5.9 0.0 copy-start.6
  5.9 0.0 copy-start.7
  5.9 26.6 %all_to_all.25.recv_ref = bf16[16,256,256]{2,1,0:T(8,128)(2,1)S(1)} all-to-all(bf16[16,256,256]{2,1,0:T(8,128)(2,1)S(1)} %shard_map.103), channel_id=1, replica_groups=mesh['y'=4,'x'=4,'z_hi'=16,'z_lo'=2,'core'=2] {'y','x'}, dimensions={0} | all-to-all | bytes 4194304 | tf_op jit(solution)/shard_map/all_to_all | solution.py:125
  32.5 0.0 copy-done.4
  32.5 0.0 copy-done.5
  32.5 0.0 copy-done.6
  32.5 0.0 copy-done.7
  32.5 1.2 shard_map.104
  33.7 0.0 copy-start
  33.7 1.3 copy-done
  35.0 25.0 %all_to_all.26.in_ref = bf16[64,16,128]{2,1,0:T(8,128)(2,1)S(1)} all-to-all(bf16[64,16,128]{2,1,0:T(8,128)(2,1)S(1)} %get-tuple-element.10), channel_id=1, replica_groups=mesh['y'=4,'x'=4,'z_hi'=16,'z_lo'=2,'core'=2] {'y','x','z_lo','core'}, dimensions={0} | all-to-all | bytes 524288 | tf_op jit(solution)/shard_map/all_to_all | solution.py:139
  60.0 0.1 shard_map.106
  60.1 48.6 %all_to_all.27.in_ref = bf16[16,16,128]{2,1,0:T(8,128)(2,1)S(1)} all-to-all(bf16[16,16,128]{2,1,0:T(8,128)(2,1)S(1)} %shard_map.106), channel_id=1, replica_groups=mesh['y'=4,'x'=4,'z_hi'=16,'z_lo'=2,'core'=2] {'z_hi'}, dimensions={0} | all-to-all | bytes 131072 | tf_op jit(solution)/shard_map/all_to_all | solution.py:142
  108.6 0.0 copy-start.2
  108.6 0.0 copy-start.9
  108.6 0.0 copy-start.11
  108.6 3.8 %all-to-all-start.1 = ((bf16[16,256,256]{2,1,0:T(8,128)(2,1)}), bf16[16,256,256]{2,1,0:T(8,128)(2,1)S(1)}, u32[]{:S(2)}, u32[]{:S(2)}) async-start(bf16[16,256,256]{2,1,0:T(8,128)(2,1)} %copy-done), calls=%async_computation.1 | async-start | bytes 4194304 | tf_op jit(solution)/shard_map/all_to_all | solution.py:141
  112.5 0.7 shard_map.107
  113.2 24.5 %all-to-all-done.1.every_ref = bf16[16,256,256]{2,1,0:T(8,128)(2,1)S(1)} async-done(((bf16[16,256,256]{2,1,0:T(8,128)(2,1)}), bf16[16,256,256]{2,1,0:T(8,128)(2,1)S(1)}, u32[]{:S(2)}, u32[]{:S(2)}) %all-to-all-start.1) | async-done | bytes 2097184 | tf_op jit(solution)/shard_map/all_to_all | solution.py:141
  137.8 9.8 %all-to-all-start.4 = ((bf16[64,16,128]{2,1,0:T(8,128)(2,1)}), bf16[64,16,128]{2,1,0:T(8,128)(2,1)S(1)}, u32[]{:S(2)}, u32[]{:S(2)}) async-start(bf16[64,16,128]{2,1,0:T(8,128)(2,1)} %shard_map.107), calls=%async_computation.4 | async-start | bytes 524288 | tf_op jit(solution)/shard_map/all_to_all | solution.py:144
  147.6 0.0 copy-done.2
  147.6 0.0 copy-done.9
  147.6 0.0 copy-done.11
  147.6 1.8 %shard_map.105 = bf16[256,256]{1,0:T(8,128)(2,1)} custom-call(s32[16]{0:T(128)S(1)} %copy-done.9, s32[16,1]{1,0:T(8,128)S(1)} %copy.11.peer_ref, s32[16]{0:T(128)S(1)} %copy-done.11, bf16[16,128,128]{2,1,0:T(8,128)(2,1)S(1)} %copy-done.2, bf16[16,256,256]{2,1,0:T(8,128)(2,1)S(1)} %all-to-all-done.1.every_ref, f32[256,256]{1,0:T(8,128)S(1)} %get-tuple-element.9.base_ref), custom_call_target="tpu_custom_call" | custom-call | flops 134217728 | bytes 3145728 | tf_op jit(solution)/shard_map/pallas_call | solution.py:145
  149.4 8.2 %all-to-all-done.4.in_ref = bf16[64,16,128]{2,1,0:T(8,128)(2,1)S(1)} async-done(((bf16[64,16,128]{2,1,0:T(8,128)(2,1)}), bf16[64,16,128]{2,1,0:T(8,128)(2,1)S(1)}, u32[]{:S(2)}, u32[]{:S(2)}) %all-to-all-start.4) | async-done | bytes 262176 | tf_op jit(solution)/shard_map/all_to_all | solution.py:144
  157.7 0.8 shard_map.108
Async XLA Ops:
  1.4 1.0 copy-start.1
  2.4 0.9 copy-start.3
  3.3 0.7 copy-start.8
  4.0 0.7 copy-start.10
  5.9 26.6 %copy-start.4 = (bf16[256,256]{1,0:T(8,128)(2,1)S(1)}, bf16[256,256]{1,0:T(8,128)(2,1)}, u32[]{:S(2)}) copy-start(bf16[256,256]{1,0:T(8,128)(2,1)} %feat_ref.3) | copy-start | bytes 393220
  5.9 26.6 %copy-start.5 = (bf16[256,256]{1,0:T(8,128)(2,1)S(1)}, bf16[256,256]{1,0:T(8,128)(2,1)}, u32[]{:S(2)}) copy-start(bf16[256,256]{1,0:T(8,128)(2,1)} %ws_ref.1) | copy-start | bytes 393220
  5.9 26.6 %copy-start.6 = (bf16[256,256]{1,0:T(8,128)(2,1)S(1)}, bf16[256,256]{1,0:T(8,128)(2,1)}, u32[]{:S(2)}) copy-start(bf16[256,256]{1,0:T(8,128)(2,1)} %wn_ref.1) | copy-start | bytes 393220
  5.9 26.6 %copy-start.7 = (bf16[256,256]{1,0:T(8,128)(2,1)S(1)}, bf16[256,256]{1,0:T(8,128)(2,1)}, u32[]{:S(2)}) copy-start(bf16[256,256]{1,0:T(8,128)(2,1)} %grad_ref.1) | copy-start | bytes 393220
  33.7 1.3 copy-start
  108.6 39.0 %copy-start.2 = (bf16[16,128,128]{2,1,0:T(8,128)(2,1)S(1)}, bf16[16,128,128]{2,1,0:T(8,128)(2,1)}, u32[]{:S(2)}) copy-start(bf16[16,128,128]{2,1,0:T(8,128)(2,1)} %adj_ref.3) | copy-start | bytes 1572868
  108.6 39.0 %copy-start.9 = (s32[16]{0:T(128)S(1)}, s32[16]{0:T(128)}, u32[]{:S(2)}) copy-start(s32[16]{0:T(128)} %src_ref.3) | copy-start | bytes 196
  108.6 39.0 %copy-start.11 = (s32[16]{0:T(128)S(1)}, s32[16]{0:T(128)}, u32[]{:S(2)}) copy-start(s32[16]{0:T(128)} %dst_ref.3) | copy-start | bytes 196
  108.6 29.1 %all-to-all-start.1 = ((bf16[16,256,256]{2,1,0:T(8,128)(2,1)}), bf16[16,256,256]{2,1,0:T(8,128)(2,1)S(1)}, u32[]{:S(2)}, u32[]{:S(2)}) async-start(bf16[16,256,256]{2,1,0:T(8,128)(2,1)} %copy-done), calls=%async_computation.1 | async-start | bytes 4194304 | tf_op jit(solution)/shard_map/all_to_all | solution.py:141
  137.8 19.9 %all-to-all-start.4 = ((bf16[64,16,128]{2,1,0:T(8,128)(2,1)}), bf16[64,16,128]{2,1,0:T(8,128)(2,1)S(1)}, u32[]{:S(2)}, u32[]{:S(2)}) async-start(bf16[64,16,128]{2,1,0:T(8,128)(2,1)} %shard_map.107), calls=%async_computation.4 | async-start | bytes 524288 | tf_op jit(solution)/shard_map/all_to_all | solution.py:144

commit v2 on v1

--- a/solution.py
+++ b/solution.py
@@ -51,7 +51,7 @@
         src = pl.multiple_of(src_ref[t] * tile, tile)
         dst = pl.multiple_of(dst_ref[t] * tile, tile)
         prod = jnp.dot(adj_ref[t], feat_ref[pl.ds(src, tile), :], preferred_element_type=F32)
-        where = (peer_ref[t, 0], pl.ds(dst, tile), slice(None))
+        where = (peer_ref[t], pl.ds(dst, tile), slice(None))
         out_ref[where] = (out_ref[where].astype(F32) + prod.astype(BF16).astype(F32)).astype(BF16)
 
 
@@ -75,19 +75,24 @@
         part = part.reshape(half, rows // 2, width)
         part = jnp.concatenate([part[:, :, :lanes], part[:, :, lanes:]], axis=1)
         wg_ref[k * half : (k + 1) * half] = part.astype(BF16)
-    agg_grad = lax.dot_general(dpre, wn_ref[...], NT, preferred_element_type=F32).astype(BF16)
-    for p in range(peers):
-        agg_grad_ref[p] = agg_grad
+    agg_grad_ref[...] = lax.dot_general(
+        dpre, wn_ref[...], NT, preferred_element_type=F32
+    ).astype(BF16)
     base_ref[...] = lax.dot_general(dpre, ws_ref[...], NT, preferred_element_type=F32)
 
 
-def gradient(src_ref, peer_ref, dst_ref, adj_ref, every_ref, base_ref, out_ref, acc_ref):
+def gradient(
+    src_ref, peer_ref, dst_ref, adj_ref, base_ref, s0, s1, s2, s3, out_ref, acc_ref, every_ref
+):
     count, tile, _ = adj_ref.shape
+    wide = s0.shape[0]
+    for k, stack in enumerate((s0, s1, s2, s3)):
+        every_ref[k * wide : (k + 1) * wide] = stack[...]
     acc_ref[...] = base_ref[...]
     for t in range(count):
         src = pl.multiple_of(src_ref[t] * tile, tile)
         dst = pl.multiple_of(dst_ref[t] * tile, tile)
-        picked = every_ref[peer_ref[t, 0], pl.ds(dst, tile), :]
+        picked = every_ref[peer_ref[t], pl.ds(dst, tile), :]
         acc_ref[pl.ds(src, tile), :] += lax.dot_general(
             adj_ref[t], picked, TN, preferred_element_type=F32
         )
@@ -107,6 +112,11 @@
     out_ref[...] = got.reshape(out_ref.shape)
 
 
+def from_ahead(value, axis, step):
+    n = lax.axis_size(axis)
+    return lax.ppermute(value, axis, [((i + step) % n, i) for i in range(n)])
+
+
 def body(features, adjacency, src_tile, dst_peer, dst_tile, w_self, w_neigh, out_grad):
     nodes, width = features.shape
     count, tile, _ = adjacency.shape
@@ -114,6 +124,11 @@
     near, far = lax.axis_size(NEAR), lax.axis_size(FAR)
     total_nodes = nodes * lax.axis_size(ALL)
     rows = 2 * width * width // near // 128
+    peer = dst_peer.reshape(count)
+    n_y, n_x = lax.axis_size("y"), lax.axis_size("x")
+    ahead = (peer // n_x - lax.axis_index("y")) % n_y * n_x + (
+        peer % n_x - lax.axis_index("x")
+    ) % n_x
     dense = call(
         partial_sums,
         shape((parts, nodes, width), BF16),
@@ -121,14 +136,14 @@
         2,
         flops=2 * count * tile * tile * width,
         size=3 << 20,
-    )(src_tile, dst_peer, dst_tile, features, adjacency)
+    )(src_tile, peer, dst_tile, features, adjacency)
     recv = lax.all_to_all(dense, LINE, 0, 0)
     output, base, mine, wgrad = call(
         layer,
         (
             shape((nodes, width), BF16),
             shape((nodes, width), F32),
-            shape((parts, nodes, width), BF16),
+            shape((nodes, width), BF16),
             shape((near, rows, 128), BF16),
         ),
         0,
@@ -137,20 +152,24 @@
         size=5 << 20,
     )(recv, features, w_self, w_neigh, out_grad)
     wgrad = lax.all_to_all(wgrad, NEAR, 0, 0)
+    line = [mine] + [from_ahead(mine, "x", k) for k in range(1, n_x)]
+    wgrad, line = lax.optimization_barrier((wgrad, line))
     wgrad = call(spread_sum, shape((far, rows, 128), BF16), 0, 1, size=1 << 19)(wgrad)
-    every = lax.all_to_all(mine, LINE, 0, 0)
     wgrad = lax.all_to_all(wgrad, FAR, 0, 0)
+    line = jnp.stack(line)
+    stacks = [line] + [from_ahead(line, "y", k) for k in range(1, n_y)]
+    wgrad, stacks = lax.optimization_barrier((wgrad, stacks))
     wgrad = call(spread_sum, shape((near, rows, 128), BF16), 0, 1, size=1 << 19)(wgrad)
     wgrad = lax.all_to_all(wgrad, NEAR, 0, 0)
     feat_grad = call(
         gradient,
         shape((nodes, width), BF16),
         3,
-        3,
-        scratch=[pltpu.VMEM((nodes, width), F32)],
+        2 + n_y,
+        scratch=[pltpu.VMEM((nodes, width), F32), pltpu.VMEM((parts, nodes, width), BF16)],
         flops=2 * count * tile * tile * width,
         size=3 << 20,
-    )(src_tile, dst_peer, dst_tile, adjacency, every, base)
+    )(src_tile, ahead, dst_tile, adjacency, base, *stacks)
 
     def last(in_ref, out_ref):
         unpack(in_ref, out_ref, scale=1.0 / math.sqrt(total_nodes))

time: 159 us -> 144 us (0.906)
  starting transfers between devices: 13.6 us -> 42.1 us
  blocking collectives: 100 us -> 75.8 us
  waiting for transfers between devices: 32.8 us -> 14.3 us
    all_to_all x1 -> x0, blocking collectives: 25 us -> none  [body(): wgrad = lax.all_to_all(wgrad, NEAR, 0, 0)]
    all_to_all x1 -> x0, waiting for transfers between devices: 24.5 us -> none  [body(): every = lax.all_to_all(mine, LINE, 0, 0)]
    ppermute x0 -> x6, starting transfers between devices: none -> 18.9 us  [from_ahead(): return lax.ppermute(value, axis, [((i + step) % n, i) for i in range(n)])]
    all_to_all x1 -> x2, starting transfers between devices: 9.8 us -> 23.2 us  [body(): wgrad = lax.all_to_all(wgrad, NEAR, 0, 0)]
    ppermute x0 -> x6, waiting for transfers between devices: none -> 6.15 us  [from_ahead(): return lax.ppermute(value, axis, [((i + step) % n, i) for i in range(n)])]
    all_to_all x1 -> x0, starting transfers between devices: 3.85 us -> none  [body(): every = lax.all_to_all(mine, LINE, 0, 0)]
    unnamed x25 -> x26, local copies, waits for them, and re-layouts: 5.35 us -> 3.94 us
    all_to_all x1 -> x2, waiting for transfers between devices: 8.25 us -> 8.12 us  [body(): wgrad = lax.all_to_all(wgrad, NEAR, 0, 0)]
  transfers between devices with their start and end apart: 2 -> 8, of which waited for: 2 -> 3; matrix products, arithmetic and copies ran while one was open for 0% -> 0% of each run, Pallas kernels for 2% -> 1%
where the time goes in v2:
time: 144 us; the launch traced here: 143 us
  blocking collectives  75.8 us (53%)
  starting transfers between devices  42.1 us (29%)
  waiting for transfers between devices  14.3 us (10%)
  Pallas kernels  6.02 us (4%)
  local copies, waits for them, and re-layouts  3.94 us (3%)
    all_to_all x1, blocking collectives, body(): wgrad = lax.all_to_all(wgrad, FAR, 0, 0)  49.2 us
    all_to_all x1, blocking collectives, body(): recv = lax.all_to_all(dense, LINE, 0, 0)  26.6 us
    all_to_all x2, starting transfers between devices, body(): wgrad = lax.all_to_all(wgrad, NEAR, 0, 0)  23.2 us
    ppermute x6, starting transfers between devices, from_ahead(): return lax.ppermute(value, axis, [((i + step) % n, i) for i in range(n)])  18.9 us
    all_to_all x2, waiting for transfers between devices, body(): wgrad = lax.all_to_all(wgrad, NEAR, 0, 0)  8.12 us
    ppermute x6, waiting for transfers between devices, from_ahead(): return lax.ppermute(value, axis, [((i + step) % n, i) for i in range(n)])  6.15 us
    unnamed x26, local copies, waits for them, and re-layouts  3.94 us
  transfers between devices with their start and end apart: 8, of which 3 were waited for; matrix products, arithmetic and copies ran while one was open for 0% of the time, Pallas kernels for 1%

profile of v2, /device:TPU:1, one launch (start us, length us, event | category | flops | bytes accessed | tf_op | source)
XLA Modules:
  0.0 143.0 jit_solution(12024979527645394445)
XLA Ops:
  0.6 0.0 copy-start
  0.6 1.0 copy-done
  1.7 0.0 copy-start.2
  1.7 0.9 copy-done.2
  2.6 0.0 copy-start.7
  2.6 0.7 copy-done.7
  3.2 0.0 copy-start.9
  3.2 0.7 copy-done.9
  3.9 0.0 copy-start.11
  3.9 0.7 copy-done.11
  4.5 1.1 shard_map.103
  5.7 0.0 copy-start.3
  5.7 0.0 copy-start.4
  5.7 0.0 copy-start.5
  5.7 0.0 copy-start.6
  5.7 26.6 %all_to_all.20.recv_ref = bf16[16,256,256]{2,1,0:T(8,128)(2,1)S(1)} all-to-all(bf16[16,256,256]{2,1,0:T(8,128)(2,1)S(1)} %shard_map.103), channel_id=1, replica_groups=mesh['y'=4,'x'=4,'z_hi'=16,'z_lo'=2,'core'=2] {'y','x'}, dimensions={0} | all-to-all | bytes 4194304 | tf_op jit(solution)/shard_map/all_to_all | solution.py:140
  32.3 0.0 copy-done.3
  32.3 0.0 copy-done.4
  32.3 0.0 copy-done.5
  32.3 0.0 copy-done.6
  32.3 1.5 %shard_map.104 = (bf16[256,256]{1,0:T(8,128)(2,1)}, f32[256,256]{1,0:T(8,128)S(1)}, bf16[256,256]{1,0:T(8,128)(2,1)S(1)}, bf16[64,16,128]{2,1,0:T(8,128)(2,1)}) custom-call(bf16[16,256,256]{2,1,0:T(8,128)(2,1)S(1)} %all_to_all.20.recv_ref, bf16[256,256]{1,0:T(8,128)(2,1)S(1)} %copy-done.3, bf16[256,256]{1,0:T(8,128)(2,1)S(1)} %copy-done.4, ...), custom_call_target="tpu_custom_call" | custom-call | flops 201326592 | bytes 5242880 | tf_op jit(solution)/shard_map/pallas_call | solution.py:141
  33.8 0.0 copy-start.12
  33.8 15.4 %all-to-all-start.1 = ((bf16[64,16,128]{2,1,0:T(8,128)(2,1)}), bf16[64,16,128]{2,1,0:T(8,128)(2,1)S(1)}, u32[]{:S(2)}, u32[]{:S(2)}) async-start(bf16[64,16,128]{2,1,0:T(8,128)(2,1)} %get-tuple-element.19), calls=%async_computation.1 | async-start | bytes 524288 | tf_op jit(solution)/shard_map/all_to_all | solution.py:154
  49.2 4.5 %collective-permute-start = (bf16[256,256]{1,0:T(8,128)(2,1)S(1)}, bf16[256,256]{1,0:T(8,128)(2,1)S(1)}, u32[]{:S(2)}, u32[]{:S(2)}) collective-permute-start(bf16[256,256]{1,0:T(8,128)(2,1)S(1)} %get-tuple-element.22), channel_id=1, source_target_pairs={{64,0},{128,64},{192,128},{0,192},{65,1},{129,65},{193,129},{1,193... | collective-permute-start | bytes 393224 | tf_op jit(solution)/shard_map/ppermute | solution.py:117
  53.7 2.5 %collective-permute-start.1 = (bf16[256,256]{1,0:T(8,128)(2,1)S(1)}, bf16[256,256]{1,0:T(8,128)(2,1)S(1)}, u32[]{:S(2)}, u32[]{:S(2)}) collective-permute-start(bf16[256,256]{1,0:T(8,128)(2,1)S(1)} %get-tuple-element.22), channel_id=1, source_target_pairs={{128,0},{192,64},{0,128},{64,192},{129,1},{193,65},{1,129},{65,193... | collective-permute-start | bytes 393224 | tf_op jit(solution)/shard_map/ppermute | solution.py:117
  56.2 2.5 %collective-permute-start.2 = (bf16[256,256]{1,0:T(8,128)(2,1)S(1)}, bf16[256,256]{1,0:T(8,128)(2,1)S(1)}, u32[]{:S(2)}, u32[]{:S(2)}) collective-permute-start(bf16[256,256]{1,0:T(8,128)(2,1)S(1)} %get-tuple-element.22), channel_id=1, source_target_pairs={{192,0},{0,64},{64,128},{128,192},{193,1},{1,65},{65,129},{129,193... | collective-permute-start | bytes 393224 | tf_op jit(solution)/shard_map/ppermute | solution.py:117
  58.7 0.0 collective-permute-done
  58.7 2.8 %collective-permute-done.1 = bf16[256,256]{1,0:T(8,128)(2,1)S(1)} collective-permute-done((bf16[256,256]{1,0:T(8,128)(2,1)S(1)}, bf16[256,256]{1,0:T(8,128)(2,1)S(1)}, u32[]{:S(2)}, u32[]{:S(2)}) %collective-permute-start.1) | collective-permute-done | bytes 131104 | tf_op jit(solution)/shard_map/ppermute | solution.py:117
  61.5 3.3 %collective-permute-done.2 = bf16[256,256]{1,0:T(8,128)(2,1)S(1)} collective-permute-done((bf16[256,256]{1,0:T(8,128)(2,1)S(1)}, bf16[256,256]{1,0:T(8,128)(2,1)S(1)}, u32[]{:S(2)}, u32[]{:S(2)}) %collective-permute-start.2) | collective-permute-done | bytes 131104 | tf_op jit(solution)/shard_map/ppermute | solution.py:117
  64.8 0.0 all-to-all-done.1.in_ref
  64.8 0.1 pad_maximum_fusion.s0
  64.9 4.6 %collective-permute-start.3 = (bf16[4,256,256]{2,1,0:T(8,128)(2,1)S(1)}, bf16[4,256,256]{2,1,0:T(8,128)(2,1)S(1)}, u32[]{:S(2)}, u32[]{:S(2)}) collective-permute-start(bf16[4,256,256]{2,1,0:T(8,128)(2,1)S(1)} %pad_maximum_fusion.s0), channel_id=1, source_target_pairs={{256,0},{512,256},{768,512},{0,768},{257,1},{513,257},{769,513},{1... | collective-permute-start | bytes 1572872 | tf_op jit(solution)/shard_map/ppermute | solution.py:117
  69.5 2.3 %collective-permute-start.4 = (bf16[4,256,256]{2,1,0:T(8,128)(2,1)S(1)}, bf16[4,256,256]{2,1,0:T(8,128)(2,1)S(1)}, u32[]{:S(2)}, u32[]{:S(2)}) collective-permute-start(bf16[4,256,256]{2,1,0:T(8,128)(2,1)S(1)} %pad_maximum_fusion.s0), channel_id=1, source_target_pairs={{512,0},{768,256},{0,512},{256,768},{513,1},{769,257},{1,513},{257... | collective-permute-start | bytes 1572872 | tf_op jit(solution)/shard_map/ppermute | solution.py:117
  71.7 2.6 %collective-permute-start.5 = (bf16[4,256,256]{2,1,0:T(8,128)(2,1)S(1)}, bf16[4,256,256]{2,1,0:T(8,128)(2,1)S(1)}, u32[]{:S(2)}, u32[]{:S(2)}) collective-permute-start(bf16[4,256,256]{2,1,0:T(8,128)(2,1)S(1)} %pad_maximum_fusion.s0), channel_id=1, source_target_pairs={{768,0},{0,256},{256,512},{512,768},{769,1},{1,257},{257,513},{513... | collective-permute-start | bytes 1572872 | tf_op jit(solution)/shard_map/ppermute | solution.py:117
  74.3 0.1 shard_map.105
  74.4 49.2 %all_to_all.21.in_ref = bf16[16,16,128]{2,1,0:T(8,128)(2,1)S(1)} all-to-all(bf16[16,16,128]{2,1,0:T(8,128)(2,1)S(1)} %shard_map.105), channel_id=1, replica_groups=mesh['y'=4,'x'=4,'z_hi'=16,'z_lo'=2,'core'=2] {'z_hi'}, dimensions={0} | all-to-all | bytes 131072 | tf_op jit(solution)/shard_map/all_to_all | solution.py:158
  123.6 0.0 collective-permute-done.3.s1
  123.6 0.0 collective-permute-done.4.s2
  123.6 0.0 collective-permute-done.5.s3
  123.6 0.7 shard_map.107
  124.4 7.8 %all-to-all-start.3 = ((bf16[64,16,128]{2,1,0:T(8,128)(2,1)}), bf16[64,16,128]{2,1,0:T(8,128)(2,1)S(1)}, u32[]{:S(2)}, u32[]{:S(2)}) async-start(bf16[64,16,128]{2,1,0:T(8,128)(2,1)} %shard_map.107), calls=%async_computation.3 | async-start | bytes 524288 | tf_op jit(solution)/shard_map/all_to_all | solution.py:163
  132.2 0.0 copy-done.12
  132.2 0.0 copy-done.1
  132.2 0.0 copy-done.8
  132.3 0.0 copy-done.10
  132.3 1.8 %shard_map.106 = bf16[256,256]{1,0:T(8,128)(2,1)} custom-call(s32[16]{0:T(128)S(1)} %copy-done.8, s32[16]{0:T(128)S(1)} %fusion.peer_ref, s32[16]{0:T(128)S(1)} %copy-done.10, bf16[16,128,128]{2,1,0:T(8,128)(2,1)S(1)} %copy-done.1, f32[256,256]{1,0:T(8,128)S(1)} %get-tuple-element.18.base_ref, bf16[4,256,256]{2,1,0:T(8,128)(2,1)S(1)} %pad_maximum_fusion.s0, ...), custom_call_target="tpu_custom_call" | custom-call | flops 134217728 | bytes 3145728 | tf_op jit(solution)/shard_map/pallas_call | solution.py:164
  134.1 8.1 %all-to-all-done.3.in_ref = bf16[64,16,128]{2,1,0:T(8,128)(2,1)S(1)} async-done(((bf16[64,16,128]{2,1,0:T(8,128)(2,1)}), bf16[64,16,128]{2,1,0:T(8,128)(2,1)S(1)}, u32[]{:S(2)}, u32[]{:S(2)}) %all-to-all-start.3) | async-done | bytes 262176 | tf_op jit(solution)/shard_map/all_to_all | solution.py:163
  142.2 0.8 shard_map.108
  (4 shorter events, 0.0 us)
Async XLA Ops:
  0.6 1.0 copy-start
  1.7 0.9 copy-start.2
  2.6 0.7 copy-start.7
  3.2 0.7 copy-start.9
  3.9 0.7 copy-start.11
  5.7 26.6 %copy-start.3 = (bf16[256,256]{1,0:T(8,128)(2,1)S(1)}, bf16[256,256]{1,0:T(8,128)(2,1)}, u32[]{:S(2)}) copy-start(bf16[256,256]{1,0:T(8,128)(2,1)} %feat_ref.3) | copy-start | bytes 393220
  5.7 26.6 %copy-start.4 = (bf16[256,256]{1,0:T(8,128)(2,1)S(1)}, bf16[256,256]{1,0:T(8,128)(2,1)}, u32[]{:S(2)}) copy-start(bf16[256,256]{1,0:T(8,128)(2,1)} %ws_ref.1) | copy-start | bytes 393220
  5.7 26.6 %copy-start.5 = (bf16[256,256]{1,0:T(8,128)(2,1)S(1)}, bf16[256,256]{1,0:T(8,128)(2,1)}, u32[]{:S(2)}) copy-start(bf16[256,256]{1,0:T(8,128)(2,1)} %wn_ref.1) | copy-start | bytes 393220
  5.7 26.6 %copy-start.6 = (bf16[256,256]{1,0:T(8,128)(2,1)S(1)}, bf16[256,256]{1,0:T(8,128)(2,1)}, u32[]{:S(2)}) copy-start(bf16[256,256]{1,0:T(8,128)(2,1)} %grad_ref.1) | copy-start | bytes 393220
  33.8 98.4 %copy-start.12 = (s32[16,1]{0,1:T(1,128)S(1)}, s32[16,1]{0,1:T(1,128)}, u32[]{:S(2)}) copy-start(s32[16,1]{0,1:T(1,128)} %param.11) | copy-start | bytes 196
  33.8 98.5 %copy-start.1 = (bf16[16,128,128]{2,1,0:T(8,128)(2,1)S(1)}, bf16[16,128,128]{2,1,0:T(8,128)(2,1)}, u32[]{:S(2)}) copy-start(bf16[16,128,128]{2,1,0:T(8,128)(2,1)} %adj_ref.3) | copy-start | bytes 1572868
  33.8 98.5 %copy-start.8 = (s32[16]{0:T(128)S(1)}, s32[16]{0:T(128)}, u32[]{:S(2)}) copy-start(s32[16]{0:T(128)} %src_ref.3) | copy-start | bytes 196
  33.8 98.5 %copy-start.10 = (s32[16]{0:T(128)S(1)}, s32[16]{0:T(128)}, u32[]{:S(2)}) copy-start(s32[16]{0:T(128)} %dst_ref.3) | copy-start | bytes 196
  33.8 31.0 %all-to-all-start.1 = ((bf16[64,16,128]{2,1,0:T(8,128)(2,1)}), bf16[64,16,128]{2,1,0:T(8,128)(2,1)S(1)}, u32[]{:S(2)}, u32[]{:S(2)}) async-start(bf16[64,16,128]{2,1,0:T(8,128)(2,1)} %get-tuple-element.19), calls=%async_computation.1 | async-start | bytes 524288 | tf_op jit(solution)/shard_map/all_to_all | solution.py:154
  49.2 9.5 %collective-permute-start = (bf16[256,256]{1,0:T(8,128)(2,1)S(1)}, bf16[256,256]{1,0:T(8,128)(2,1)S(1)}, u32[]{:S(2)}, u32[]{:S(2)}) collective-permute-start(bf16[256,256]{1,0:T(8,128)(2,1)S(1)} %get-tuple-element.22), channel_id=1, source_target_pairs={{64,0},{128,64},{192,128},{0,192},{65,1},{129,65},{193,129},{1,193... | collective-permute-start | bytes 393224 | tf_op jit(solution)/shard_map/ppermute | solution.py:117
  53.7 7.8 %collective-permute-start.1 = (bf16[256,256]{1,0:T(8,128)(2,1)S(1)}, bf16[256,256]{1,0:T(8,128)(2,1)S(1)}, u32[]{:S(2)}, u32[]{:S(2)}) collective-permute-start(bf16[256,256]{1,0:T(8,128)(2,1)S(1)} %get-tuple-element.22), channel_id=1, source_target_pairs={{128,0},{192,64},{0,128},{64,192},{129,1},{193,65},{1,129},{65,193... | collective-permute-start | bytes 393224 | tf_op jit(solution)/shard_map/ppermute | solution.py:117
  56.2 8.6 %collective-permute-start.2 = (bf16[256,256]{1,0:T(8,128)(2,1)S(1)}, bf16[256,256]{1,0:T(8,128)(2,1)S(1)}, u32[]{:S(2)}, u32[]{:S(2)}) collective-permute-start(bf16[256,256]{1,0:T(8,128)(2,1)S(1)} %get-tuple-element.22), channel_id=1, source_target_pairs={{192,0},{0,64},{64,128},{128,192},{193,1},{1,65},{65,129},{129,193... | collective-permute-start | bytes 393224 | tf_op jit(solution)/shard_map/ppermute | solution.py:117
  64.9 58.7 %collective-permute-start.3 = (bf16[4,256,256]{2,1,0:T(8,128)(2,1)S(1)}, bf16[4,256,256]{2,1,0:T(8,128)(2,1)S(1)}, u32[]{:S(2)}, u32[]{:S(2)}) collective-permute-start(bf16[4,256,256]{2,1,0:T(8,128)(2,1)S(1)} %pad_maximum_fusion.s0), channel_id=1, source_target_pairs={{256,0},{512,256},{768,512},{0,768},{257,1},{513,257},{769,513},{1... | collective-permute-start | bytes 1572872 | tf_op jit(solution)/shard_map/ppermute | solution.py:117
  69.5 54.2 %collective-permute-start.4 = (bf16[4,256,256]{2,1,0:T(8,128)(2,1)S(1)}, bf16[4,256,256]{2,1,0:T(8,128)(2,1)S(1)}, u32[]{:S(2)}, u32[]{:S(2)}) collective-permute-start(bf16[4,256,256]{2,1,0:T(8,128)(2,1)S(1)} %pad_maximum_fusion.s0), channel_id=1, source_target_pairs={{512,0},{768,256},{0,512},{256,768},{513,1},{769,257},{1,513},{257... | collective-permute-start | bytes 1572872 | tf_op jit(solution)/shard_map/ppermute | solution.py:117
  71.7 51.9 %collective-permute-start.5 = (bf16[4,256,256]{2,1,0:T(8,128)(2,1)S(1)}, bf16[4,256,256]{2,1,0:T(8,128)(2,1)S(1)}, u32[]{:S(2)}, u32[]{:S(2)}) collective-permute-start(bf16[4,256,256]{2,1,0:T(8,128)(2,1)S(1)} %pad_maximum_fusion.s0), channel_id=1, source_target_pairs={{768,0},{0,256},{256,512},{512,768},{769,1},{1,257},{257,513},{513... | collective-permute-start | bytes 1572872 | tf_op jit(solution)/shard_map/ppermute | solution.py:117
  124.4 17.8 %all-to-all-start.3 = ((bf16[64,16,128]{2,1,0:T(8,128)(2,1)}), bf16[64,16,128]{2,1,0:T(8,128)(2,1)S(1)}, u32[]{:S(2)}, u32[]{:S(2)}) async-start(bf16[64,16,128]{2,1,0:T(8,128)(2,1)} %shard_map.107), calls=%async_computation.3 | async-start | bytes 524288 | tf_op jit(solution)/shard_map/all_to_all | solution.py:163

commit v3 on v2

--- a/solution.py
+++ b/solution.py
@@ -13,6 +13,7 @@
 Z_LO = 2
 LINE = ("y", "x")
 NEAR = ("y", "x", "z_lo", "core")
+REST = ("y", "z_lo", "core")
 FAR = "z_hi"
 ALL = ("y", "x", "z_hi", "z_lo", "core")
 TN = (((0,), (0,)), ((), ()))
@@ -44,9 +45,17 @@
     return jax.ShapeDtypeStruct(dims, dtype)
 
 
-def partial_sums(src_ref, peer_ref, dst_ref, feat_ref, adj_ref, out_ref):
+def partial_sums(
+    src_in, peer_in, dst_in, feat_in, adj_in, out_ref, src_ref, peer_ref, dst_ref, feat_ref, adj_ref, sems
+):
+    pairs = ((src_in, src_ref), (peer_in, peer_ref), (dst_in, dst_ref), (feat_in, feat_ref), (adj_in, adj_ref))
+    copies = [pltpu.make_async_copy(a, b, sems.at[k]) for k, (a, b) in enumerate(pairs)]
+    for copy in reversed(copies):
+        copy.start()
     count, tile, _ = adj_ref.shape
     out_ref[...] = jnp.zeros_like(out_ref)
+    for copy in copies:
+        copy.wait()
     for t in range(count):
         src = pl.multiple_of(src_ref[t] * tile, tile)
         dst = pl.multiple_of(dst_ref[t] * tile, tile)
@@ -55,7 +64,7 @@
         out_ref[where] = (out_ref[where].astype(F32) + prod.astype(BF16).astype(F32)).astype(BF16)
 
 
-def layer(recv_ref, feat_ref, ws_ref, wn_ref, grad_ref, out_ref, base_ref, agg_grad_ref, wg_ref):
+def layer(recv_ref, feat_ref, ws_ref, wn_ref, grad_ref, out_ref, base_ref, sent_ref):
     peers, nodes, width = recv_ref.shape
     agg = recv_ref[0].astype(F32)
     for p in range(1, peers):
@@ -68,16 +77,18 @@
     sig = jax.nn.sigmoid(pre)
     out_ref[...] = (pre * sig).astype(BF16)
     dpre = (grad_ref[...].astype(F32) * sig * (1.0 + pre * (1.0 - sig))).astype(BF16)
-    chunks, rows, lanes = wg_ref.shape
-    half = chunks // 2
+    agg_grad = lax.dot_general(dpre, wn_ref[...], NT, preferred_element_type=F32).astype(BF16)
+    n_x, length, _ = sent_ref.shape
+    share = (length - nodes) // (2 * 2)
     for k, left in enumerate((feat, low)):
-        part = lax.dot_general(left, dpre, TN, preferred_element_type=F32)
-        part = part.reshape(half, rows // 2, width)
-        part = jnp.concatenate([part[:, :, :lanes], part[:, :, lanes:]], axis=1)
-        wg_ref[k * half : (k + 1) * half] = part.astype(BF16)
-    agg_grad_ref[...] = lax.dot_general(
-        dpre, wn_ref[...], NT, preferred_element_type=F32
-    ).astype(BF16)
+        part = lax.dot_general(left, dpre, TN, preferred_element_type=F32).astype(BF16)
+        part = part.reshape(2, n_x, share, width)
+        for x in range(n_x):
+            for y in range(2):
+                at = nodes + (2 * k + y) * share
+                sent_ref[x, at : at + share] = part[y, x]
+    for x in range(n_x):
+        sent_ref[x, :nodes] = agg_grad
     base_ref[...] = lax.dot_general(dpre, ws_ref[...], NT, preferred_element_type=F32)
 
 
@@ -99,6 +110,14 @@
     out_ref[...] = acc_ref[...].astype(BF16)
 
 
+def split_line(in_ref, line_ref, wg_ref):
+    nodes, width = line_ref.shape[1:]
+    chunks, rows, lanes = wg_ref.shape
+    line_ref[...] = in_ref[:, :nodes]
+    part = jnp.sum(in_ref[:, nodes:].astype(F32), axis=0).reshape(chunks, rows // 2, width)
+    wg_ref[...] = jnp.concatenate([part[:, :, :lanes], part[:, :, lanes:]], axis=1).astype(BF16)
+
+
 def spread_sum(in_ref, out_ref):
     total = jnp.sum(in_ref[...].astype(F32), axis=0).astype(out_ref.dtype)
     for p in range(out_ref.shape[0]):
@@ -126,38 +145,45 @@
     rows = 2 * width * width // near // 128
     peer = dst_peer.reshape(count)
     n_y, n_x = lax.axis_size("y"), lax.axis_size("x")
-    ahead = (peer // n_x - lax.axis_index("y")) % n_y * n_x + (
-        peer % n_x - lax.axis_index("x")
-    ) % n_x
-    dense = call(
+    ahead = (peer // n_x - lax.axis_index("y")) % n_y * n_x + peer % n_x
+    dense = pl.pallas_call(
         partial_sums,
-        shape((parts, nodes, width), BF16),
-        3,
-        2,
-        flops=2 * count * tile * tile * width,
-        size=3 << 20,
+        out_shape=shape((parts, nodes, width), BF16),
+        in_specs=[pl.BlockSpec(memory_space=pltpu.HBM)] * 5,
+        out_specs=vmem(),
+        scratch_shapes=[pltpu.SMEM((count,), jnp.int32)] * 3
+        + [pltpu.VMEM((nodes, width), BF16), pltpu.VMEM((count, tile, tile), BF16)]
+        + [pltpu.SemaphoreType.DMA((5,))],
+        compiler_params=pltpu.CompilerParams(vmem_limit_bytes=60 << 20),
+        cost_estimate=pl.CostEstimate(
+            flops=2 * count * tile * tile * width, bytes_accessed=3 << 20, transcendentals=0
+        ),
     )(src_tile, peer, dst_tile, features, adjacency)
     recv = lax.all_to_all(dense, LINE, 0, 0)
-    output, base, mine, wgrad = call(
+    output, base, sent = call(
         layer,
         (
             shape((nodes, width), BF16),
             shape((nodes, width), F32),
-            shape((nodes, width), BF16),
-            shape((near, rows, 128), BF16),
+            shape((n_x, nodes + 2 * width // n_x, width), BF16),
         ),
         0,
         5,
         flops=12 * nodes * width * width,
         size=5 << 20,
     )(recv, features, w_self, w_neigh, out_grad)
-    wgrad = lax.all_to_all(wgrad, NEAR, 0, 0)
-    line = [mine] + [from_ahead(mine, "x", k) for k in range(1, n_x)]
-    wgrad, line = lax.optimization_barrier((wgrad, line))
+    sent = lax.all_to_all(sent, "x", 0, 0)
+    line, wgrad = call(
+        split_line,
+        (shape((n_x, nodes, width), BF16), shape((near // n_x, rows, 128), BF16)),
+        0,
+        1,
+        size=1 << 20,
+    )(sent)
+    wgrad = lax.all_to_all(wgrad, REST, 0, 0)
+    stacks = [line] + [from_ahead(line, "y", k) for k in range(1, n_y)]
     wgrad = call(spread_sum, shape((far, rows, 128), BF16), 0, 1, size=1 << 19)(wgrad)
     wgrad = lax.all_to_all(wgrad, FAR, 0, 0)
-    line = jnp.stack(line)
-    stacks = [line] + [from_ahead(line, "y", k) for k in range(1, n_y)]
     wgrad, stacks = lax.optimization_barrier((wgrad, stacks))
     wgrad = call(spread_sum, shape((near, rows, 128), BF16), 0, 1, size=1 << 19)(wgrad)
     wgrad = lax.all_to_all(wgrad, NEAR, 0, 0)

time: 144 us -> 140 us (0.972)
  blocking collectives: 75.8 us -> 37.8 us
  starting transfers between devices: 42.1 us -> 62.3 us
  waiting for transfers between devices: 14.3 us -> 30 us
  local copies, waits for them, and re-layouts: 3.94 us -> 0.04 us
  Pallas kernels: 6.02 us -> 8.82 us
    all_to_all x0 -> x2, starting transfers between devices: none -> 44.6 us  [the longest x1 27.5 us: body(): wgrad = lax.all_to_all(wgrad, FAR, 0, 0)]
    all_to_all x1, blocking collectives: 49.2 us -> 11.4 us  [body(): sent = lax.all_to_all(sent, 'x', 0, 0)]
    all_to_all x0 -> x2, waiting for transfers between devices: none -> 21.9 us  [the longest x1 21.9 us: body(): wgrad = lax.all_to_all(wgrad, FAR, 0, 0)]
    all_to_all x2 -> x1, starting transfers between devices: 23.2 us -> 8.32 us  [body(): wgrad = lax.all_to_all(wgrad, NEAR, 0, 0)]
    ppermute x6 -> x3, starting transfers between devices: 18.9 us -> 9.47 us  [from_ahead(): return lax.ppermute(value, axis, [((i + step) % n, i) for i in range(n)])]
    ppermute x6 -> x3, waiting for transfers between devices: 6.15 us -> 0.01 us  [from_ahead(): return lax.ppermute(value, axis, [((i + step) % n, i) for i in range(n)])]
    unnamed x26 -> x16, local copies, waits for them, and re-layouts: 3.94 us -> 0.04 us
    pallas_call x1 -> x2, Pallas kernels: 1.12 us -> 3.61 us  [the longest x1 2.94 us: body(): pl.pallas_call(partial_sums, out_shape=shape((parts, nodes, width), BF16)...]
  transfers between devices with their start and end apart: 8 -> 6, of which waited for: 3 -> 2; matrix products, arithmetic and copies ran while one was open for 0% -> 0% of each run, Pallas kernels for 1% -> 2%
where the time goes in v3:
time: 140 us
  starting transfers between devices  62.3 us (44%)
  blocking collectives  37.8 us (27%)
  waiting for transfers between devices  30 us (21%)
  Pallas kernels  8.82 us (6%)
    all_to_all x1, starting transfers between devices, body(): wgrad = lax.all_to_all(wgrad, FAR, 0, 0)  27.5 us
    all_to_all x1, blocking collectives, body(): recv = lax.all_to_all(dense, LINE, 0, 0)  26.4 us
    all_to_all x1, waiting for transfers between devices, body(): wgrad = lax.all_to_all(wgrad, FAR, 0, 0)  21.9 us
    all_to_all x1, starting transfers between devices, body(): wgrad = lax.all_to_all(wgrad, REST, 0, 0)  17 us
    all_to_all x1, blocking collectives, body(): sent = lax.all_to_all(sent, 'x', 0, 0)  11.4 us
    ppermute x3, starting transfers between devices, from_ahead(): return lax.ppermute(value, axis, [((i + step) % n, i) for i in range(n)])  9.47 us
    all_to_all x1, starting transfers between devices, body(): wgrad = lax.all_to_all(wgrad, NEAR, 0, 0)  8.32 us
    all_to_all x1, waiting for transfers between devices, body(): wgrad = lax.all_to_all(wgrad, NEAR, 0, 0)  8.11 us
  transfers between devices with their start and end apart: 6, of which 2 were waited for; matrix products, arithmetic and copies ran while one was open for 0% of the time, Pallas kernels for 2%

profile of v3, /device:TPU:1, one launch (start us, length us, event | category | flops | bytes accessed | tf_op | source)
XLA Modules:
  0.0 139.9 jit_solution(9871688655331437234)
XLA Ops:
  0.6 2.9 %shard_map.103 = bf16[16,256,256]{2,1,0:T(8,128)(2,1)} custom-call(s32[16]{0:T(128)} %src_ref.1, s32[16]{0:T(128)} %bitcast.2, s32[16]{0:T(128)} %dst_ref.1, bf16[256,256]{1,0:T(8,128)(2,1)} %feat_ref.1, bf16[16,128,128]{2,1,0:T(8,128)(2,1)} %adj_ref.1), custom_call_target="tpu_custom_call" | custom-call | flops 134217728 | bytes 3145728 | tf_op jit(solution)/shard_map/pallas_call | solution.py:149
  3.6 0.0 copy-start.1
  3.6 0.0 copy-start.2
  3.6 0.0 copy-start.3
  3.6 0.0 copy-start.4
  3.6 26.4 %all_to_all.25.recv_ref = bf16[16,256,256]{2,1,0:T(8,128)(2,1)S(1)} all-to-all(bf16[16,256,256]{2,1,0:T(8,128)(2,1)} %shard_map.103), channel_id=1, replica_groups=mesh['y'=4,'x'=4,'z_hi'=16,'z_lo'=2,'core'=2] {'y','x'}, dimensions={0} | all-to-all | bytes 4194304 | tf_op jit(solution)/shard_map/all_to_all | solution.py:162
  30.1 0.0 copy-done.1
  30.1 0.0 copy-done.2
  30.1 0.0 copy-done.3
  30.1 0.0 copy-done.4
  30.1 1.2 shard_map.104
  31.3 0.0 copy-start.7
  31.3 0.0 copy-start
  31.3 0.0 copy-start.5
  31.3 0.0 copy-start.6
  31.3 11.4 %all_to_all.26.in_ref = bf16[4,384,256]{2,1,0:T(8,128)(2,1)S(1)} all-to-all(bf16[4,384,256]{2,1,0:T(8,128)(2,1)S(1)} %get-tuple-element.15), channel_id=1, replica_groups=mesh['y'=4,'x'=4,'z_hi'=16,'z_lo'=2,'core'=2] {'x'}, dimensions={0} | all-to-all | bytes 1572864 | tf_op jit(solution)/shard_map/all_to_all | solution.py:175
  42.6 0.7 shard_map.105
  43.3 17.0 %all-to-all-start.2 = ((bf16[16,16,128]{2,1,0:T(8,128)(2,1)}), bf16[16,16,128]{2,1,0:T(8,128)(2,1)S(1)}, u32[]{:S(2)}, u32[]{:S(2)}) async-start(bf16[16,16,128]{2,1,0:T(8,128)(2,1)} %get-tuple-element.16), calls=%async_computation.2 | async-start | bytes 131072 | tf_op jit(solution)/shard_map/all_to_all | solution.py:183
  60.3 4.5 %collective-permute-start = (bf16[4,256,256]{2,1,0:T(8,128)(2,1)S(1)}, bf16[4,256,256]{2,1,0:T(8,128)(2,1)S(1)}, u32[]{:S(2)}, u32[]{:S(2)}) collective-permute-start(bf16[4,256,256]{2,1,0:T(8,128)(2,1)S(1)} %get-tuple-element.18.s0), channel_id=1, source_target_pairs={{256,0},{512,256},{768,512},{0,768},{257,1},{513,257},{769,513},{1... | collective-permute-start | bytes 1572872 | tf_op jit(solution)/shard_map/ppermute | solution.py:136
  64.9 2.5 %collective-permute-start.1 = (bf16[4,256,256]{2,1,0:T(8,128)(2,1)S(1)}, bf16[4,256,256]{2,1,0:T(8,128)(2,1)S(1)}, u32[]{:S(2)}, u32[]{:S(2)}) collective-permute-start(bf16[4,256,256]{2,1,0:T(8,128)(2,1)S(1)} %get-tuple-element.18.s0), channel_id=1, source_target_pairs={{512,0},{768,256},{0,512},{256,768},{513,1},{769,257},{1,513},{257... | collective-permute-start | bytes 1572872 | tf_op jit(solution)/shard_map/ppermute | solution.py:136
  67.3 2.5 %collective-permute-start.2 = (bf16[4,256,256]{2,1,0:T(8,128)(2,1)S(1)}, bf16[4,256,256]{2,1,0:T(8,128)(2,1)S(1)}, u32[]{:S(2)}, u32[]{:S(2)}) collective-permute-start(bf16[4,256,256]{2,1,0:T(8,128)(2,1)S(1)} %get-tuple-element.18.s0), channel_id=1, source_target_pairs={{768,0},{0,256},{256,512},{512,768},{769,1},{1,257},{257,513},{513... | collective-permute-start | bytes 1572872 | tf_op jit(solution)/shard_map/ppermute | solution.py:136
  69.8 0.0 all-to-all-done.2.in_ref
  69.8 0.7 shard_map.106
  70.5 27.5 %all-to-all-start.3 = ((bf16[16,16,128]{2,1,0:T(8,128)(2,1)}), bf16[16,16,128]{2,1,0:T(8,128)(2,1)S(1)}, u32[]{:S(2)}, u32[]{:S(2)}) async-start(bf16[16,16,128]{2,1,0:T(8,128)(2,1)} %shard_map.106), calls=%async_computation.3 | async-start | bytes 131072 | tf_op jit(solution)/shard_map/all_to_all | solution.py:186
  98.0 0.0 collective-permute-done.s1
  98.0 0.0 collective-permute-done.1.s2
  98.1 0.0 collective-permute-done.2.s3
  98.1 21.9 %all-to-all-done.3.in_ref = bf16[16,16,128]{2,1,0:T(8,128)(2,1)S(1)} async-done(((bf16[16,16,128]{2,1,0:T(8,128)(2,1)}), bf16[16,16,128]{2,1,0:T(8,128)(2,1)S(1)}, u32[]{:S(2)}, u32[]{:S(2)}) %all-to-all-start.3) | async-done | bytes 65568 | tf_op jit(solution)/shard_map/all_to_all | solution.py:186
  120.0 0.7 shard_map.108
  120.7 8.3 %all-to-all-start.4 = ((bf16[64,16,128]{2,1,0:T(8,128)(2,1)}), bf16[64,16,128]{2,1,0:T(8,128)(2,1)S(1)}, u32[]{:S(2)}, u32[]{:S(2)}) async-start(bf16[64,16,128]{2,1,0:T(8,128)(2,1)} %shard_map.108), calls=%async_computation.4 | async-start | bytes 524288 | tf_op jit(solution)/shard_map/all_to_all | solution.py:189
  129.0 0.0 copy-done.7
  129.1 0.0 copy-done
  129.1 0.0 copy-done.5
  129.1 0.0 copy-done.6
  129.1 1.8 %shard_map.107 = bf16[256,256]{1,0:T(8,128)(2,1)} custom-call(s32[16]{0:T(128)S(1)} %copy-done.5, s32[16]{0:T(128)S(1)} %fusion.peer_ref, s32[16]{0:T(128)S(1)} %copy-done.6, bf16[16,128,128]{2,1,0:T(8,128)(2,1)S(1)} %copy-done, f32[256,256]{1,0:T(8,128)S(1)} %get-tuple-element.14.base_ref, bf16[4,256,256]{2,1,0:T(8,128)(2,1)S(1)} %get-tuple-element.18.s0, ...), custom_call_target="tpu_custom_call" | custom-call | flops 134217728 | bytes 3145728 | tf_op jit(solution)/shard_map/pallas_call | solution.py:190
  130.9 8.1 %all-to-all-done.4.in_ref = bf16[64,16,128]{2,1,0:T(8,128)(2,1)S(1)} async-done(((bf16[64,16,128]{2,1,0:T(8,128)(2,1)}), bf16[64,16,128]{2,1,0:T(8,128)(2,1)S(1)}, u32[]{:S(2)}, u32[]{:S(2)}) %all-to-all-start.4) | async-done | bytes 262176 | tf_op jit(solution)/shard_map/all_to_all | solution.py:189
  139.0 0.8 shard_map.109
  (1 shorter events, 0.0 us)
Async XLA Ops:
  3.6 26.5 %copy-start.1 = (bf16[256,256]{1,0:T(8,128)(2,1)S(1)}, bf16[256,256]{1,0:T(8,128)(2,1)}, u32[]{:S(2)}) copy-start(bf16[256,256]{1,0:T(8,128)(2,1)} %feat_ref.1) | copy-start | bytes 393220
  3.6 26.5 %copy-start.2 = (bf16[256,256]{1,0:T(8,128)(2,1)S(1)}, bf16[256,256]{1,0:T(8,128)(2,1)}, u32[]{:S(2)}) copy-start(bf16[256,256]{1,0:T(8,128)(2,1)} %ws_ref.1) | copy-start | bytes 393220
  3.6 26.5 %copy-start.3 = (bf16[256,256]{1,0:T(8,128)(2,1)S(1)}, bf16[256,256]{1,0:T(8,128)(2,1)}, u32[]{:S(2)}) copy-start(bf16[256,256]{1,0:T(8,128)(2,1)} %wn_ref.1) | copy-start | bytes 393220
  3.6 26.5 %copy-start.4 = (bf16[256,256]{1,0:T(8,128)(2,1)S(1)}, bf16[256,256]{1,0:T(8,128)(2,1)}, u32[]{:S(2)}) copy-start(bf16[256,256]{1,0:T(8,128)(2,1)} %grad_ref.1) | copy-start | bytes 393220
  31.3 97.8 %copy-start.7 = (s32[16,1]{0,1:T(1,128)S(1)}, s32[16,1]{0,1:T(1,128)}, u32[]{:S(2)}) copy-start(s32[16,1]{0,1:T(1,128)} %param.11) | copy-start | bytes 196
  31.3 97.8 %copy-start = (bf16[16,128,128]{2,1,0:T(8,128)(2,1)S(1)}, bf16[16,128,128]{2,1,0:T(8,128)(2,1)}, u32[]{:S(2)}) copy-start(bf16[16,128,128]{2,1,0:T(8,128)(2,1)} %adj_ref.1) | copy-start | bytes 1572868
  31.3 97.8 %copy-start.5 = (s32[16]{0:T(128)S(1)}, s32[16]{0:T(128)}, u32[]{:S(2)}) copy-start(s32[16]{0:T(128)} %src_ref.1) | copy-start | bytes 196
  31.3 97.8 %copy-start.6 = (s32[16]{0:T(128)S(1)}, s32[16]{0:T(128)}, u32[]{:S(2)}) copy-start(s32[16]{0:T(128)} %dst_ref.1) | copy-start | bytes 196
  43.3 26.5 %all-to-all-start.2 = ((bf16[16,16,128]{2,1,0:T(8,128)(2,1)}), bf16[16,16,128]{2,1,0:T(8,128)(2,1)S(1)}, u32[]{:S(2)}, u32[]{:S(2)}) async-start(bf16[16,16,128]{2,1,0:T(8,128)(2,1)} %get-tuple-element.16), calls=%async_computation.2 | async-start | bytes 131072 | tf_op jit(solution)/shard_map/all_to_all | solution.py:183
  60.3 37.7 %collective-permute-start = (bf16[4,256,256]{2,1,0:T(8,128)(2,1)S(1)}, bf16[4,256,256]{2,1,0:T(8,128)(2,1)S(1)}, u32[]{:S(2)}, u32[]{:S(2)}) collective-permute-start(bf16[4,256,256]{2,1,0:T(8,128)(2,1)S(1)} %get-tuple-element.18.s0), channel_id=1, source_target_pairs={{256,0},{512,256},{768,512},{0,768},{257,1},{513,257},{769,513},{1... | collective-permute-start | bytes 1572872 | tf_op jit(solution)/shard_map/ppermute | solution.py:136
  64.9 33.2 %collective-permute-start.1 = (bf16[4,256,256]{2,1,0:T(8,128)(2,1)S(1)}, bf16[4,256,256]{2,1,0:T(8,128)(2,1)S(1)}, u32[]{:S(2)}, u32[]{:S(2)}) collective-permute-start(bf16[4,256,256]{2,1,0:T(8,128)(2,1)S(1)} %get-tuple-element.18.s0), channel_id=1, source_target_pairs={{512,0},{768,256},{0,512},{256,768},{513,1},{769,257},{1,513},{257... | collective-permute-start | bytes 1572872 | tf_op jit(solution)/shard_map/ppermute | solution.py:136
  67.3 30.7 %collective-permute-start.2 = (bf16[4,256,256]{2,1,0:T(8,128)(2,1)S(1)}, bf16[4,256,256]{2,1,0:T(8,128)(2,1)S(1)}, u32[]{:S(2)}, u32[]{:S(2)}) collective-permute-start(bf16[4,256,256]{2,1,0:T(8,128)(2,1)S(1)} %get-tuple-element.18.s0), channel_id=1, source_target_pairs={{768,0},{0,256},{256,512},{512,768},{769,1},{1,257},{257,513},{513... | collective-permute-start | bytes 1572872 | tf_op jit(solution)/shard_map/ppermute | solution.py:136
  70.5 49.5 %all-to-all-start.3 = ((bf16[16,16,128]{2,1,0:T(8,128)(2,1)}), bf16[16,16,128]{2,1,0:T(8,128)(2,1)S(1)}, u32[]{:S(2)}, u32[]{:S(2)}) async-start(bf16[16,16,128]{2,1,0:T(8,128)(2,1)} %shard_map.106), calls=%async_computation.3 | async-start | bytes 131072 | tf_op jit(solution)/shard_map/all_to_all | solution.py:186
  120.7 18.3 %all-to-all-start.4 = ((bf16[64,16,128]{2,1,0:T(8,128)(2,1)}), bf16[64,16,128]{2,1,0:T(8,128)(2,1)S(1)}, u32[]{:S(2)}, u32[]{:S(2)}) async-start(bf16[64,16,128]{2,1,0:T(8,128)(2,1)} %shard_map.108), calls=%async_computation.4 | async-start | bytes 524288 | tf_op jit(solution)/shard_map/all_to_all | solution.py:189

commit v4 on v3

--- a/solution.py
+++ b/solution.py
@@ -1,3 +1,4 @@
+import functools
 import math
 
 import jax
@@ -46,8 +47,9 @@
 
 
 def partial_sums(
-    src_in, peer_in, dst_in, feat_in, adj_in, out_ref, src_ref, peer_ref, dst_ref, feat_ref, adj_ref, sems
+    src_in, peer_in, dst_in, feat_in, adj_in, out_ref, src_ref, peer_ref, dst_ref, feat_ref, adj_ref, sems, *, lead
 ):
+    parts = out_ref.shape[0]
     pairs = ((src_in, src_ref), (peer_in, peer_ref), (dst_in, dst_ref), (feat_in, feat_ref), (adj_in, adj_ref))
     copies = [pltpu.make_async_copy(a, b, sems.at[k]) for k, (a, b) in enumerate(pairs)]
     for copy in reversed(copies):
@@ -60,7 +62,7 @@
         src = pl.multiple_of(src_ref[t] * tile, tile)
         dst = pl.multiple_of(dst_ref[t] * tile, tile)
         prod = jnp.dot(adj_ref[t], feat_ref[pl.ds(src, tile), :], preferred_element_type=F32)
-        where = (peer_ref[t], pl.ds(dst, tile), slice(None))
+        where = (lax.rem(peer_ref[t] + (parts - lead), parts), pl.ds(dst, tile), slice(None))
         out_ref[where] = (out_ref[where].astype(F32) + prod.astype(BF16).astype(F32)).astype(BF16)
 
 
@@ -131,6 +133,10 @@
     out_ref[...] = got.reshape(out_ref.shape)
 
 
+def led_by(first, count):
+    return [(first + k) % count for k in range(count)]
+
+
 def from_ahead(value, axis, step):
     n = lax.axis_size(axis)
     return lax.ppermute(value, axis, [((i + step) % n, i) for i in range(n)])
@@ -144,10 +150,11 @@
     total_nodes = nodes * lax.axis_size(ALL)
     rows = 2 * width * width // near // 128
     peer = dst_peer.reshape(count)
+    lead = parts * 10 // 16
     n_y, n_x = lax.axis_size("y"), lax.axis_size("x")
     ahead = (peer // n_x - lax.axis_index("y")) % n_y * n_x + peer % n_x
     dense = pl.pallas_call(
-        partial_sums,
+        functools.partial(partial_sums, lead=lead),
         out_shape=shape((parts, nodes, width), BF16),
         in_specs=[pl.BlockSpec(memory_space=pltpu.HBM)] * 5,
         out_specs=vmem(),
@@ -159,7 +166,7 @@
             flops=2 * count * tile * tile * width, bytes_accessed=3 << 20, transcendentals=0
         ),
     )(src_tile, peer, dst_tile, features, adjacency)
-    recv = lax.all_to_all(dense, LINE, 0, 0)
+    recv = lax.all_to_all(dense, LINE, 0, 0, axis_index_groups=[led_by(lead, parts)])
     output, base, sent = call(
         layer,
         (
@@ -183,7 +190,7 @@
     wgrad = lax.all_to_all(wgrad, REST, 0, 0)
     stacks = [line] + [from_ahead(line, "y", k) for k in range(1, n_y)]
     wgrad = call(spread_sum, shape((far, rows, 128), BF16), 0, 1, size=1 << 19)(wgrad)
-    wgrad = lax.all_to_all(wgrad, FAR, 0, 0)
+    wgrad = lax.all_to_all(wgrad, FAR, 0, 0, axis_index_groups=[led_by(far * 10 // 16, far)])
     wgrad, stacks = lax.optimization_barrier((wgrad, stacks))
     wgrad = call(spread_sum, shape((near, rows, 128), BF16), 0, 1, size=1 << 19)(wgrad)
     wgrad = lax.all_to_all(wgrad, NEAR, 0, 0)

time: 140 us -> 129 us (0.921)
  waiting for transfers between devices: 30 us -> 16.3 us
  starting transfers between devices: 62.3 us -> 64.9 us
    all_to_all x1, waiting for transfers between devices: 21.9 us -> 8.2 us  [body(): lax.all_to_all(wgrad, FAR, 0, 0, axis_index_groups=[led_by(far * 10 // 16...]
    all_to_all x1, blocking collectives: 26.4 us -> 23 us  [body(): lax.all_to_all(dense, LINE, 0, 0, axis_index_groups=[led_by(lead, parts)])]
    all_to_all x1, blocking collectives: 11.4 us -> 14.5 us  [body(): sent = lax.all_to_all(sent, 'x', 0, 0)]
    all_to_all x1, starting transfers between devices: 17 us -> 18.8 us  [body(): wgrad = lax.all_to_all(wgrad, REST, 0, 0)]
where the time goes in v4:
time: 129 us; the launch traced here: 128 us
  starting transfers between devices  64.9 us (50%)
  blocking collectives  37.5 us (29%)
  waiting for transfers between devices  16.3 us (13%)
  Pallas kernels  8.82 us (7%)
    all_to_all x1, starting transfers between devices, body(): lax.all_to_all(wgrad, FAR, 0, 0, axis_index_groups=[led_by(far * 10 // 16...  27.5 us
    all_to_all x1, blocking collectives, body(): lax.all_to_all(dense, LINE, 0, 0, axis_index_groups=[led_by(lead, parts)])  23 us
    all_to_all x1, starting transfers between devices, body(): wgrad = lax.all_to_all(wgrad, REST, 0, 0)  18.8 us
    all_to_all x1, blocking collectives, body(): sent = lax.all_to_all(sent, 'x', 0, 0)  14.5 us
    ppermute x3, starting transfers between devices, from_ahead(): return lax.ppermute(value, axis, [((i + step) % n, i) for i in range(n)])  9.51 us
    all_to_all x1, starting transfers between devices, body(): wgrad = lax.all_to_all(wgrad, NEAR, 0, 0)  9.1 us
    all_to_all x1, waiting for transfers between devices, body(): lax.all_to_all(wgrad, FAR, 0, 0, axis_index_groups=[led_by(far * 10 // 16...  8.2 us
    all_to_all x1, waiting for transfers between devices, body(): wgrad = lax.all_to_all(wgrad, NEAR, 0, 0)  8.11 us
  transfers between devices with their start and end apart: 6, of which 2 were waited for; matrix products, arithmetic and copies ran while one was open for 0% of the time, Pallas kernels for 2%

profile of v4, /device:TPU:1, one launch (start us, length us, event | category | flops | bytes accessed | tf_op | source)
XLA Modules:
  0.0 128.4 jit_solution(11907627272205612723)
XLA Ops:
  0.6 2.9 %shard_map.103 = bf16[16,256,256]{2,1,0:T(8,128)(2,1)} custom-call(s32[16]{0:T(128)} %src_ref.1, s32[16]{0:T(128)} %bitcast.2, s32[16]{0:T(128)} %dst_ref.1, bf16[256,256]{1,0:T(8,128)(2,1)} %feat_ref.1, bf16[16,128,128]{2,1,0:T(8,128)(2,1)} %adj_ref.1), custom_call_target="tpu_custom_call" | custom-call | flops 134217728 | bytes 3145728 | tf_op jit(solution)/shard_map/pallas_call | solution.py:156
  3.6 0.0 copy-start.1
  3.6 0.0 copy-start.2
  3.6 0.0 copy-start.3
  3.6 0.0 copy-start.4
  3.6 23.0 %all_to_all.25.recv_ref = bf16[16,256,256]{2,1,0:T(8,128)(2,1)S(1)} all-to-all(bf16[16,256,256]{2,1,0:T(8,128)(2,1)} %shard_map.103), channel_id=1, replica_groups={{640,704,768,832,896,960,0,64,128,192,256,320,384,448,512,576},{641,705..., dimensions={0} | all-to-all | bytes 4194304 | tf_op jit(solution)/shard_map/all_to_all | solution.py:169
  26.6 0.0 copy-done.1
  26.6 0.0 copy-done.2
  26.6 0.0 copy-done.3
  26.6 0.0 copy-done.4
  26.6 1.2 shard_map.104
  27.8 0.0 copy-start.7
  27.8 0.0 copy-start
  27.8 0.0 copy-start.5
  27.8 0.0 copy-start.6
  27.8 14.5 %all_to_all.26.in_ref = bf16[4,384,256]{2,1,0:T(8,128)(2,1)S(1)} all-to-all(bf16[4,384,256]{2,1,0:T(8,128)(2,1)S(1)} %get-tuple-element.15), channel_id=1, replica_groups=mesh['y'=4,'x'=4,'z_hi'=16,'z_lo'=2,'core'=2] {'x'}, dimensions={0} | all-to-all | bytes 1572864 | tf_op jit(solution)/shard_map/all_to_all | solution.py:182
  42.3 0.7 shard_map.105
  43.0 18.8 %all-to-all-start.2 = ((bf16[16,16,128]{2,1,0:T(8,128)(2,1)}), bf16[16,16,128]{2,1,0:T(8,128)(2,1)S(1)}, u32[]{:S(2)}, u32[]{:S(2)}) async-start(bf16[16,16,128]{2,1,0:T(8,128)(2,1)} %get-tuple-element.16), calls=%async_computation.2 | async-start | bytes 131072 | tf_op jit(solution)/shard_map/all_to_all | solution.py:190
  61.8 4.6 %collective-permute-start = (bf16[4,256,256]{2,1,0:T(8,128)(2,1)S(1)}, bf16[4,256,256]{2,1,0:T(8,128)(2,1)S(1)}, u32[]{:S(2)}, u32[]{:S(2)}) collective-permute-start(bf16[4,256,256]{2,1,0:T(8,128)(2,1)S(1)} %get-tuple-element.18.s0), channel_id=1, source_target_pairs={{256,0},{512,256},{768,512},{0,768},{257,1},{513,257},{769,513},{1... | collective-permute-start | bytes 1572872 | tf_op jit(solution)/shard_map/ppermute | solution.py:142
  66.4 2.4 %collective-permute-start.1 = (bf16[4,256,256]{2,1,0:T(8,128)(2,1)S(1)}, bf16[4,256,256]{2,1,0:T(8,128)(2,1)S(1)}, u32[]{:S(2)}, u32[]{:S(2)}) collective-permute-start(bf16[4,256,256]{2,1,0:T(8,128)(2,1)S(1)} %get-tuple-element.18.s0), channel_id=1, source_target_pairs={{512,0},{768,256},{0,512},{256,768},{513,1},{769,257},{1,513},{257... | collective-permute-start | bytes 1572872 | tf_op jit(solution)/shard_map/ppermute | solution.py:142
  68.8 2.5 %collective-permute-start.2 = (bf16[4,256,256]{2,1,0:T(8,128)(2,1)S(1)}, bf16[4,256,256]{2,1,0:T(8,128)(2,1)S(1)}, u32[]{:S(2)}, u32[]{:S(2)}) collective-permute-start(bf16[4,256,256]{2,1,0:T(8,128)(2,1)S(1)} %get-tuple-element.18.s0), channel_id=1, source_target_pairs={{768,0},{0,256},{256,512},{512,768},{769,1},{1,257},{257,513},{513... | collective-permute-start | bytes 1572872 | tf_op jit(solution)/shard_map/ppermute | solution.py:142
  71.3 0.0 all-to-all-done.2.in_ref
  71.4 0.7 shard_map.106
  72.0 27.5 %all-to-all-start.3 = ((bf16[16,16,128]{2,1,0:T(8,128)(2,1)}), bf16[16,16,128]{2,1,0:T(8,128)(2,1)S(1)}, u32[]{:S(2)}, u32[]{:S(2)}) async-start(bf16[16,16,128]{2,1,0:T(8,128)(2,1)} %shard_map.106), calls=%async_computation.3 | async-start | bytes 131072 | tf_op jit(solution)/shard_map/all_to_all | solution.py:193
  99.5 0.0 collective-permute-done.s1
  99.5 0.0 collective-permute-done.1.s2
  99.5 0.0 collective-permute-done.2.s3
  99.5 8.2 %all-to-all-done.3.in_ref = bf16[16,16,128]{2,1,0:T(8,128)(2,1)S(1)} async-done(((bf16[16,16,128]{2,1,0:T(8,128)(2,1)}), bf16[16,16,128]{2,1,0:T(8,128)(2,1)S(1)}, u32[]{:S(2)}, u32[]{:S(2)}) %all-to-all-start.3) | async-done | bytes 65568 | tf_op jit(solution)/shard_map/all_to_all | solution.py:193
  107.7 0.7 shard_map.108
  108.5 9.1 %all-to-all-start.4 = ((bf16[64,16,128]{2,1,0:T(8,128)(2,1)}), bf16[64,16,128]{2,1,0:T(8,128)(2,1)S(1)}, u32[]{:S(2)}, u32[]{:S(2)}) async-start(bf16[64,16,128]{2,1,0:T(8,128)(2,1)} %shard_map.108), calls=%async_computation.4 | async-start | bytes 524288 | tf_op jit(solution)/shard_map/all_to_all | solution.py:196
  117.6 0.0 copy-done.7
  117.6 0.0 copy-done
  117.6 0.0 copy-done.5
  117.6 0.0 copy-done.6
  117.6 1.8 %shard_map.107 = bf16[256,256]{1,0:T(8,128)(2,1)} custom-call(s32[16]{0:T(128)S(1)} %copy-done.5, s32[16]{0:T(128)S(1)} %fusion.peer_ref, s32[16]{0:T(128)S(1)} %copy-done.6, bf16[16,128,128]{2,1,0:T(8,128)(2,1)S(1)} %copy-done, f32[256,256]{1,0:T(8,128)S(1)} %get-tuple-element.14.base_ref, bf16[4,256,256]{2,1,0:T(8,128)(2,1)S(1)} %get-tuple-element.18.s0, ...), custom_call_target="tpu_custom_call" | custom-call | flops 134217728 | bytes 3145728 | tf_op jit(solution)/shard_map/pallas_call | solution.py:197
  119.4 8.1 %all-to-all-done.4.in_ref = bf16[64,16,128]{2,1,0:T(8,128)(2,1)S(1)} async-done(((bf16[64,16,128]{2,1,0:T(8,128)(2,1)}), bf16[64,16,128]{2,1,0:T(8,128)(2,1)S(1)}, u32[]{:S(2)}, u32[]{:S(2)}) %all-to-all-start.4) | async-done | bytes 262176 | tf_op jit(solution)/shard_map/all_to_all | solution.py:196
  127.5 0.8 shard_map.109
  (1 shorter events, 0.0 us)
Async XLA Ops:
  3.6 23.0 %copy-start.1 = (bf16[256,256]{1,0:T(8,128)(2,1)S(1)}, bf16[256,256]{1,0:T(8,128)(2,1)}, u32[]{:S(2)}) copy-start(bf16[256,256]{1,0:T(8,128)(2,1)} %feat_ref.1) | copy-start | bytes 393220
  3.6 23.0 %copy-start.2 = (bf16[256,256]{1,0:T(8,128)(2,1)S(1)}, bf16[256,256]{1,0:T(8,128)(2,1)}, u32[]{:S(2)}) copy-start(bf16[256,256]{1,0:T(8,128)(2,1)} %ws_ref.1) | copy-start | bytes 393220
  3.6 23.0 %copy-start.3 = (bf16[256,256]{1,0:T(8,128)(2,1)S(1)}, bf16[256,256]{1,0:T(8,128)(2,1)}, u32[]{:S(2)}) copy-start(bf16[256,256]{1,0:T(8,128)(2,1)} %wn_ref.1) | copy-start | bytes 393220
  3.6 23.0 %copy-start.4 = (bf16[256,256]{1,0:T(8,128)(2,1)S(1)}, bf16[256,256]{1,0:T(8,128)(2,1)}, u32[]{:S(2)}) copy-start(bf16[256,256]{1,0:T(8,128)(2,1)} %grad_ref.1) | copy-start | bytes 393220
  27.8 89.8 %copy-start.7 = (s32[16,1]{0,1:T(1,128)S(1)}, s32[16,1]{0,1:T(1,128)}, u32[]{:S(2)}) copy-start(s32[16,1]{0,1:T(1,128)} %param.11) | copy-start | bytes 196
  27.8 89.8 %copy-start = (bf16[16,128,128]{2,1,0:T(8,128)(2,1)S(1)}, bf16[16,128,128]{2,1,0:T(8,128)(2,1)}, u32[]{:S(2)}) copy-start(bf16[16,128,128]{2,1,0:T(8,128)(2,1)} %adj_ref.1) | copy-start | bytes 1572868
  27.8 89.8 %copy-start.5 = (s32[16]{0:T(128)S(1)}, s32[16]{0:T(128)}, u32[]{:S(2)}) copy-start(s32[16]{0:T(128)} %src_ref.1) | copy-start | bytes 196
  27.8 89.8 %copy-start.6 = (s32[16]{0:T(128)S(1)}, s32[16]{0:T(128)}, u32[]{:S(2)}) copy-start(s32[16]{0:T(128)} %dst_ref.1) | copy-start | bytes 196
  43.0 28.3 %all-to-all-start.2 = ((bf16[16,16,128]{2,1,0:T(8,128)(2,1)}), bf16[16,16,128]{2,1,0:T(8,128)(2,1)S(1)}, u32[]{:S(2)}, u32[]{:S(2)}) async-start(bf16[16,16,128]{2,1,0:T(8,128)(2,1)} %get-tuple-element.16), calls=%async_computation.2 | async-start | bytes 131072 | tf_op jit(solution)/shard_map/all_to_all | solution.py:190
  61.8 37.7 %collective-permute-start = (bf16[4,256,256]{2,1,0:T(8,128)(2,1)S(1)}, bf16[4,256,256]{2,1,0:T(8,128)(2,1)S(1)}, u32[]{:S(2)}, u32[]{:S(2)}) collective-permute-start(bf16[4,256,256]{2,1,0:T(8,128)(2,1)S(1)} %get-tuple-element.18.s0), channel_id=1, source_target_pairs={{256,0},{512,256},{768,512},{0,768},{257,1},{513,257},{769,513},{1... | collective-permute-start | bytes 1572872 | tf_op jit(solution)/shard_map/ppermute | solution.py:142
  66.4 33.1 %collective-permute-start.1 = (bf16[4,256,256]{2,1,0:T(8,128)(2,1)S(1)}, bf16[4,256,256]{2,1,0:T(8,128)(2,1)S(1)}, u32[]{:S(2)}, u32[]{:S(2)}) collective-permute-start(bf16[4,256,256]{2,1,0:T(8,128)(2,1)S(1)} %get-tuple-element.18.s0), channel_id=1, source_target_pairs={{512,0},{768,256},{0,512},{256,768},{513,1},{769,257},{1,513},{257... | collective-permute-start | bytes 1572872 | tf_op jit(solution)/shard_map/ppermute | solution.py:142
  68.8 30.7 %collective-permute-start.2 = (bf16[4,256,256]{2,1,0:T(8,128)(2,1)S(1)}, bf16[4,256,256]{2,1,0:T(8,128)(2,1)S(1)}, u32[]{:S(2)}, u32[]{:S(2)}) collective-permute-start(bf16[4,256,256]{2,1,0:T(8,128)(2,1)S(1)} %get-tuple-element.18.s0), channel_id=1, source_target_pairs={{768,0},{0,256},{256,512},{512,768},{769,1},{1,257},{257,513},{513... | collective-permute-start | bytes 1572872 | tf_op jit(solution)/shard_map/ppermute | solution.py:142
  72.0 35.7 %all-to-all-start.3 = ((bf16[16,16,128]{2,1,0:T(8,128)(2,1)}), bf16[16,16,128]{2,1,0:T(8,128)(2,1)S(1)}, u32[]{:S(2)}, u32[]{:S(2)}) async-start(bf16[16,16,128]{2,1,0:T(8,128)(2,1)} %shard_map.106), calls=%async_computation.3 | async-start | bytes 131072 | tf_op jit(solution)/shard_map/all_to_all | solution.py:193
  108.5 19.1 %all-to-all-start.4 = ((bf16[64,16,128]{2,1,0:T(8,128)(2,1)}), bf16[64,16,128]{2,1,0:T(8,128)(2,1)S(1)}, u32[]{:S(2)}, u32[]{:S(2)}) async-start(bf16[64,16,128]{2,1,0:T(8,128)(2,1)} %shard_map.108), calls=%async_computation.4 | async-start | bytes 524288 | tf_op jit(solution)/shard_map/all_to_all | solution.py:196

commit v5 on v4

--- a/solution.py
+++ b/solution.py
@@ -14,7 +14,6 @@
 Z_LO = 2
 LINE = ("y", "x")
 NEAR = ("y", "x", "z_lo", "core")
-REST = ("y", "z_lo", "core")
 FAR = "z_hi"
 ALL = ("y", "x", "z_hi", "z_lo", "core")
 TN = (((0,), (0,)), ((), ()))
@@ -66,7 +65,7 @@
         out_ref[where] = (out_ref[where].astype(F32) + prod.astype(BF16).astype(F32)).astype(BF16)
 
 
-def layer(recv_ref, feat_ref, ws_ref, wn_ref, grad_ref, out_ref, base_ref, sent_ref):
+def layer(recv_ref, feat_ref, ws_ref, wn_ref, grad_ref, out_ref, base_ref, agg_grad_ref, wg_ref):
     peers, nodes, width = recv_ref.shape
     agg = recv_ref[0].astype(F32)
     for p in range(1, peers):
@@ -80,17 +79,15 @@
     out_ref[...] = (pre * sig).astype(BF16)
     dpre = (grad_ref[...].astype(F32) * sig * (1.0 + pre * (1.0 - sig))).astype(BF16)
     agg_grad = lax.dot_general(dpre, wn_ref[...], NT, preferred_element_type=F32).astype(BF16)
-    n_x, length, _ = sent_ref.shape
-    share = (length - nodes) // (2 * 2)
+    for x in range(agg_grad_ref.shape[0]):
+        agg_grad_ref[x] = agg_grad
+    chunks, rows, lanes = wg_ref.shape
+    half = chunks // 2
     for k, left in enumerate((feat, low)):
-        part = lax.dot_general(left, dpre, TN, preferred_element_type=F32).astype(BF16)
-        part = part.reshape(2, n_x, share, width)
-        for x in range(n_x):
-            for y in range(2):
-                at = nodes + (2 * k + y) * share
-                sent_ref[x, at : at + share] = part[y, x]
-    for x in range(n_x):
-        sent_ref[x, :nodes] = agg_grad
+        part = lax.dot_general(left, dpre, TN, preferred_element_type=F32)
+        part = part.reshape(half, rows // 2, width)
+        part = jnp.concatenate([part[:, :, :lanes], part[:, :, lanes:]], axis=1)
+        wg_ref[k * half : (k + 1) * half] = part.astype(BF16)
     base_ref[...] = lax.dot_general(dpre, ws_ref[...], NT, preferred_element_type=F32)
 
 
@@ -110,14 +107,6 @@
             adj_ref[t], picked, TN, preferred_element_type=F32
         )
     out_ref[...] = acc_ref[...].astype(BF16)
-
-
-def split_line(in_ref, line_ref, wg_ref):
-    nodes, width = line_ref.shape[1:]
-    chunks, rows, lanes = wg_ref.shape
-    line_ref[...] = in_ref[:, :nodes]
-    part = jnp.sum(in_ref[:, nodes:].astype(F32), axis=0).reshape(chunks, rows // 2, width)
-    wg_ref[...] = jnp.concatenate([part[:, :, :lanes], part[:, :, lanes:]], axis=1).astype(BF16)
 
 
 def spread_sum(in_ref, out_ref):
@@ -167,33 +156,25 @@
         ),
     )(src_tile, peer, dst_tile, features, adjacency)
     recv = lax.all_to_all(dense, LINE, 0, 0, axis_index_groups=[led_by(lead, parts)])
-    output, base, sent = call(
+    output, base, line, wgrad = call(
         layer,
         (
             shape((nodes, width), BF16),
             shape((nodes, width), F32),
-            shape((n_x, nodes + 2 * width // n_x, width), BF16),
+            shape((n_x, nodes, width), BF16),
+            shape((near, rows, 128), BF16),
         ),
         0,
         5,
         flops=12 * nodes * width * width,
         size=5 << 20,
     )(recv, features, w_self, w_neigh, out_grad)
-    sent = lax.all_to_all(sent, "x", 0, 0)
-    line, wgrad = call(
-        split_line,
-        (shape((n_x, nodes, width), BF16), shape((near // n_x, rows, 128), BF16)),
-        0,
-        1,
-        size=1 << 20,
-    )(sent)
-    wgrad = lax.all_to_all(wgrad, REST, 0, 0)
+    line = lax.all_to_all(line, "x", 0, 0)
+    line, wgrad = lax.optimization_barrier((line, wgrad))
+    wgrad = lax.all_to_all(wgrad, NEAR, 0, 0)
     stacks = [line] + [from_ahead(line, "y", k) for k in range(1, n_y)]
     wgrad = call(spread_sum, shape((far, rows, 128), BF16), 0, 1, size=1 << 19)(wgrad)
     wgrad = lax.all_to_all(wgrad, FAR, 0, 0, axis_index_groups=[led_by(far * 10 // 16, far)])
-    wgrad, stacks = lax.optimization_barrier((wgrad, stacks))
-    wgrad = call(spread_sum, shape((near, rows, 128), BF16), 0, 1, size=1 << 19)(wgrad)
-    wgrad = lax.all_to_all(wgrad, NEAR, 0, 0)
     feat_grad = call(
         gradient,
         shape((nodes, width), BF16),
@@ -203,6 +184,9 @@
         flops=2 * count * tile * tile * width,
         size=3 << 20,
     )(src_tile, ahead, dst_tile, adjacency, base, *stacks)
+    wgrad, feat_grad = lax.optimization_barrier((wgrad, feat_grad))
+    wgrad = call(spread_sum, shape((near, rows, 128), BF16), 0, 1, size=1 << 19)(wgrad)
+    wgrad = lax.all_to_all(wgrad, NEAR, 0, 0)
 
     def last(in_ref, out_ref):
         unpack(in_ref, out_ref, scale=1.0 / math.sqrt(total_nodes))

time: 129 us -> 128 us (level)
  blocking collectives: 37.5 us -> 54 us
  starting transfers between devices: 64.9 us -> 55.8 us
  waiting for transfers between devices: 16.3 us -> 8.76 us
    all_to_all x1 -> x0, starting transfers between devices: 18.8 us -> none  [body(): wgrad = lax.all_to_all(wgrad, REST, 0, 0)]
    all_to_all x1 -> x2, blocking collectives: 14.5 us -> 31.1 us  [the longest x1 18.2 us: body(): wgrad = lax.all_to_all(wgrad, NEAR, 0, 0)]
    all_to_all x1, starting transfers between devices: 9.1 us -> 18.3 us  [body(): wgrad = lax.all_to_all(wgrad, NEAR, 0, 0)]
    all_to_all x1, waiting for transfers between devices: 8.11 us -> 0.39 us  [body(): wgrad = lax.all_to_all(wgrad, NEAR, 0, 0)]
  transfers between devices with their start and end apart: 6 -> 5, of which waited for: 2 -> 2; matrix products, arithmetic and copies ran while one was open for 0% -> 0% of each run, Pallas kernels for 2% -> 2%
where the time goes in v5:
time: 128 us; the launch traced here: 127 us
  starting transfers between devices  55.8 us (44%)
  blocking collectives  54 us (42%)
  waiting for transfers between devices  8.76 us (7%)
  Pallas kernels  7.74 us (6%)
    all_to_all x1, starting transfers between devices, body(): lax.all_to_all(wgrad, FAR, 0, 0, axis_index_groups=[led_by(far * 10 // 16...  27.8 us
    all_to_all x1, blocking collectives, body(): lax.all_to_all(dense, LINE, 0, 0, axis_index_groups=[led_by(lead, parts)])  23 us
    all_to_all x1, starting transfers between devices, body(): wgrad = lax.all_to_all(wgrad, NEAR, 0, 0)  18.3 us
    all_to_all x1, blocking collectives, body(): wgrad = lax.all_to_all(wgrad, NEAR, 0, 0)  18.2 us
    all_to_all x1, blocking collectives, body(): line = lax.all_to_all(line, 'x', 0, 0)  12.9 us
    ppermute x3, starting transfers between devices, from_ahead(): return lax.ppermute(value, axis, [((i + step) % n, i) for i in range(n)])  9.69 us
    all_to_all x1, waiting for transfers between devices, body(): lax.all_to_all(wgrad, FAR, 0, 0, axis_index_groups=[led_by(far * 10 // 16...  8.36 us
    pallas_call x1, Pallas kernels, body(): pl.pallas_call(functools.partial(partial_sums, lead=lead), out_shape=shap...  2.94 us
  transfers between devices with their start and end apart: 5, of which 2 were waited for; matrix products, arithmetic and copies ran while one was open for 0% of the time, Pallas kernels for 2%

profile of v5, /device:TPU:1, one launch (start us, length us, event | category | flops | bytes accessed | tf_op | source)
XLA Modules:
  0.0 127.2 jit_solution(12380593633866541209)
XLA Ops:
  0.6 2.9 %shard_map.103 = bf16[16,256,256]{2,1,0:T(8,128)(2,1)} custom-call(s32[16]{0:T(128)} %src_ref.1, s32[16]{0:T(128)} %bitcast.2, s32[16]{0:T(128)} %dst_ref.1, bf16[256,256]{1,0:T(8,128)(2,1)} %feat_ref.1, bf16[16,128,128]{2,1,0:T(8,128)(2,1)} %adj_ref.1), custom_call_target="tpu_custom_call" | custom-call | flops 134217728 | bytes 3145728 | tf_op jit(solution)/shard_map/pallas_call | solution.py:145
  3.6 0.0 copy-start.1
  3.6 0.0 copy-start.2
  3.6 0.0 copy-start.3
  3.6 0.0 copy-start.4
  3.6 23.0 %all_to_all.25.recv_ref = bf16[16,256,256]{2,1,0:T(8,128)(2,1)S(1)} all-to-all(bf16[16,256,256]{2,1,0:T(8,128)(2,1)} %shard_map.103), channel_id=1, replica_groups={{640,704,768,832,896,960,0,64,128,192,256,320,384,448,512,576},{641,705..., dimensions={0} | all-to-all | bytes 4194304 | tf_op jit(solution)/shard_map/all_to_all | solution.py:158
  26.6 0.0 copy-done.1
  26.6 0.0 copy-done.2
  26.6 0.0 copy-done.3
  26.6 0.0 copy-done.4
  26.6 0.0 copy-start.7
  26.6 0.0 copy-start
  26.6 0.0 copy-start.5
  26.6 0.0 copy-start.6
  26.6 1.4 %shard_map.104 = (bf16[256,256]{1,0:T(8,128)(2,1)}, f32[256,256]{1,0:T(8,128)S(1)}, bf16[4,256,256]{2,1,0:T(8,128)(2,1)S(1)}, bf16[64,16,128]{2,1,0:T(8,128)(2,1)}) custom-call(bf16[16,256,256]{2,1,0:T(8,128)(2,1)S(1)} %all_to_all.25.recv_ref, bf16[256,256]{1,0:T(8,128)(2,1)S(1)} %copy-done.1, bf16[256,256]{1,0:T(8,128)(2,1)S(1)} %copy-done.2, ...), custom_call_target="tpu_custom_call" | custom-call | flops 201326592 | bytes 5242880 | tf_op jit(solution)/shard_map/pallas_call | solution.py:159
  28.1 12.9 %all_to_all.26.s0 = bf16[4,256,256]{2,1,0:T(8,128)(2,1)S(1)} all-to-all(bf16[4,256,256]{2,1,0:T(8,128)(2,1)S(1)} %get-tuple-element.12), channel_id=1, replica_groups=mesh['y'=4,'x'=4,'z_hi'=16,'z_lo'=2,'core'=2] {'x'}, dimensions={0} | all-to-all | bytes 1048576 | tf_op jit(solution)/shard_map/all_to_all | solution.py:172
  40.9 18.3 %all-to-all-start.2 = ((bf16[64,16,128]{2,1,0:T(8,128)(2,1)}), bf16[64,16,128]{2,1,0:T(8,128)(2,1)S(1)}, u32[]{:S(2)}, u32[]{:S(2)}) async-start(bf16[64,16,128]{2,1,0:T(8,128)(2,1)} %get-tuple-element.14), calls=%async_computation.2 | async-start | bytes 524288 | tf_op jit(solution)/shard_map/all_to_all | solution.py:174
  59.2 4.8 %collective-permute-start = (bf16[4,256,256]{2,1,0:T(8,128)(2,1)S(1)}, bf16[4,256,256]{2,1,0:T(8,128)(2,1)S(1)}, u32[]{:S(2)}, u32[]{:S(2)}) collective-permute-start(bf16[4,256,256]{2,1,0:T(8,128)(2,1)S(1)} %all_to_all.26.s0), channel_id=1, source_target_pairs={{256,0},{512,256},{768,512},{0,768},{257,1},{513,257},{769,513},{1... | collective-permute-start | bytes 1572872 | tf_op jit(solution)/shard_map/ppermute | solution.py:131
  64.1 2.3 %collective-permute-start.1 = (bf16[4,256,256]{2,1,0:T(8,128)(2,1)S(1)}, bf16[4,256,256]{2,1,0:T(8,128)(2,1)S(1)}, u32[]{:S(2)}, u32[]{:S(2)}) collective-permute-start(bf16[4,256,256]{2,1,0:T(8,128)(2,1)S(1)} %all_to_all.26.s0), channel_id=1, source_target_pairs={{512,0},{768,256},{0,512},{256,768},{513,1},{769,257},{1,513},{257... | collective-permute-start | bytes 1572872 | tf_op jit(solution)/shard_map/ppermute | solution.py:131
  66.3 2.6 %collective-permute-start.2 = (bf16[4,256,256]{2,1,0:T(8,128)(2,1)S(1)}, bf16[4,256,256]{2,1,0:T(8,128)(2,1)S(1)}, u32[]{:S(2)}, u32[]{:S(2)}) collective-permute-start(bf16[4,256,256]{2,1,0:T(8,128)(2,1)S(1)} %all_to_all.26.s0), channel_id=1, source_target_pairs={{768,0},{0,256},{256,512},{512,768},{769,1},{1,257},{257,513},{513... | collective-permute-start | bytes 1572872 | tf_op jit(solution)/shard_map/ppermute | solution.py:131
  68.9 0.4 all-to-all-done.2.in_ref
  69.3 0.7 shard_map.105
  70.0 27.8 %all-to-all-start.3 = ((bf16[16,16,128]{2,1,0:T(8,128)(2,1)}), bf16[16,16,128]{2,1,0:T(8,128)(2,1)S(1)}, u32[]{:S(2)}, u32[]{:S(2)}) async-start(bf16[16,16,128]{2,1,0:T(8,128)(2,1)} %shard_map.105), calls=%async_computation.3 | async-start | bytes 131072 | tf_op jit(solution)/shard_map/all_to_all | solution.py:177
  97.8 0.0 copy-done.7
  97.9 0.0 collective-permute-done.s1
  97.9 0.0 collective-permute-done.1.s2
  97.9 0.0 collective-permute-done.2.s3
  97.9 0.0 copy-done
  97.9 0.0 copy-done.5
  97.9 0.0 copy-done.6
  97.9 1.8 %shard_map.106 = bf16[256,256]{1,0:T(8,128)(2,1)} custom-call(s32[16]{0:T(128)S(1)} %copy-done.5, s32[16]{0:T(128)S(1)} %fusion.peer_ref, s32[16]{0:T(128)S(1)} %copy-done.6, bf16[16,128,128]{2,1,0:T(8,128)(2,1)S(1)} %copy-done, f32[256,256]{1,0:T(8,128)S(1)} %get-tuple-element.15.base_ref, bf16[4,256,256]{2,1,0:T(8,128)(2,1)S(1)} %all_to_all.26.s0, ...), custom_call_target="tpu_custom_call" | custom-call | flops 134217728 | bytes 3145728 | tf_op jit(solution)/shard_map/pallas_call | solution.py:178
  99.7 8.4 %all-to-all-done.3.in_ref = bf16[16,16,128]{2,1,0:T(8,128)(2,1)S(1)} async-done(((bf16[16,16,128]{2,1,0:T(8,128)(2,1)}), bf16[16,16,128]{2,1,0:T(8,128)(2,1)S(1)}, u32[]{:S(2)}, u32[]{:S(2)}) %all-to-all-start.3) | async-done | bytes 65568 | tf_op jit(solution)/shard_map/all_to_all | solution.py:177
  108.1 18.2 %all_to_all.27.in_ref = bf16[64,16,128]{2,1,0:T(8,128)(2,1)S(1)} all-to-all(bf16[64,16,128]{2,1,0:T(8,128)(2,1)S(1)} %shard_map.107), channel_id=1, replica_groups=mesh['y'=4,'x'=4,'z_hi'=16,'z_lo'=2,'core'=2] {'y','x','z_lo','core'}, dimensions={0} | all-to-all | bytes 524288 | tf_op jit(solution)/shard_map/all_to_all | solution.py:189
  126.3 0.8 shard_map.108
  (2 shorter events, 0.1 us)
Async XLA Ops:
  3.6 23.0 %copy-start.1 = (bf16[256,256]{1,0:T(8,128)(2,1)S(1)}, bf16[256,256]{1,0:T(8,128)(2,1)}, u32[]{:S(2)}) copy-start(bf16[256,256]{1,0:T(8,128)(2,1)} %feat_ref.1) | copy-start | bytes 393220
  3.6 23.0 %copy-start.2 = (bf16[256,256]{1,0:T(8,128)(2,1)S(1)}, bf16[256,256]{1,0:T(8,128)(2,1)}, u32[]{:S(2)}) copy-start(bf16[256,256]{1,0:T(8,128)(2,1)} %ws_ref.1) | copy-start | bytes 393220
  3.6 23.0 %copy-start.3 = (bf16[256,256]{1,0:T(8,128)(2,1)S(1)}, bf16[256,256]{1,0:T(8,128)(2,1)}, u32[]{:S(2)}) copy-start(bf16[256,256]{1,0:T(8,128)(2,1)} %wn_ref.1) | copy-start | bytes 393220
  3.6 23.0 %copy-start.4 = (bf16[256,256]{1,0:T(8,128)(2,1)S(1)}, bf16[256,256]{1,0:T(8,128)(2,1)}, u32[]{:S(2)}) copy-start(bf16[256,256]{1,0:T(8,128)(2,1)} %grad_ref.1) | copy-start | bytes 393220
  26.6 71.2 %copy-start.7 = (s32[16,1]{0,1:T(1,128)S(1)}, s32[16,1]{0,1:T(1,128)}, u32[]{:S(2)}) copy-start(s32[16,1]{0,1:T(1,128)} %param.11) | copy-start | bytes 196
  26.6 71.3 %copy-start = (bf16[16,128,128]{2,1,0:T(8,128)(2,1)S(1)}, bf16[16,128,128]{2,1,0:T(8,128)(2,1)}, u32[]{:S(2)}) copy-start(bf16[16,128,128]{2,1,0:T(8,128)(2,1)} %adj_ref.1) | copy-start | bytes 1572868
  26.6 71.3 %copy-start.5 = (s32[16]{0:T(128)S(1)}, s32[16]{0:T(128)}, u32[]{:S(2)}) copy-start(s32[16]{0:T(128)} %src_ref.1) | copy-start | bytes 196
  26.6 71.3 %copy-start.6 = (s32[16]{0:T(128)S(1)}, s32[16]{0:T(128)}, u32[]{:S(2)}) copy-start(s32[16]{0:T(128)} %dst_ref.1) | copy-start | bytes 196
  40.9 28.4 %all-to-all-start.2 = ((bf16[64,16,128]{2,1,0:T(8,128)(2,1)}), bf16[64,16,128]{2,1,0:T(8,128)(2,1)S(1)}, u32[]{:S(2)}, u32[]{:S(2)}) async-start(bf16[64,16,128]{2,1,0:T(8,128)(2,1)} %get-tuple-element.14), calls=%async_computation.2 | async-start | bytes 524288 | tf_op jit(solution)/shard_map/all_to_all | solution.py:174
  59.2 38.6 %collective-permute-start = (bf16[4,256,256]{2,1,0:T(8,128)(2,1)S(1)}, bf16[4,256,256]{2,1,0:T(8,128)(2,1)S(1)}, u32[]{:S(2)}, u32[]{:S(2)}) collective-permute-start(bf16[4,256,256]{2,1,0:T(8,128)(2,1)S(1)} %all_to_all.26.s0), channel_id=1, source_target_pairs={{256,0},{512,256},{768,512},{0,768},{257,1},{513,257},{769,513},{1... | collective-permute-start | bytes 1572872 | tf_op jit(solution)/shard_map/ppermute | solution.py:131
  64.1 33.8 %collective-permute-start.1 = (bf16[4,256,256]{2,1,0:T(8,128)(2,1)S(1)}, bf16[4,256,256]{2,1,0:T(8,128)(2,1)S(1)}, u32[]{:S(2)}, u32[]{:S(2)}) collective-permute-start(bf16[4,256,256]{2,1,0:T(8,128)(2,1)S(1)} %all_to_all.26.s0), channel_id=1, source_target_pairs={{512,0},{768,256},{0,512},{256,768},{513,1},{769,257},{1,513},{257... | collective-permute-start | bytes 1572872 | tf_op jit(solution)/shard_map/ppermute | solution.py:131
  66.3 31.5 %collective-permute-start.2 = (bf16[4,256,256]{2,1,0:T(8,128)(2,1)S(1)}, bf16[4,256,256]{2,1,0:T(8,128)(2,1)S(1)}, u32[]{:S(2)}, u32[]{:S(2)}) collective-permute-start(bf16[4,256,256]{2,1,0:T(8,128)(2,1)S(1)} %all_to_all.26.s0), channel_id=1, source_target_pairs={{768,0},{0,256},{256,512},{512,768},{769,1},{1,257},{257,513},{513... | collective-permute-start | bytes 1572872 | tf_op jit(solution)/shard_map/ppermute | solution.py:131
  70.0 38.0 %all-to-all-start.3 = ((bf16[16,16,128]{2,1,0:T(8,128)(2,1)}), bf16[16,16,128]{2,1,0:T(8,128)(2,1)S(1)}, u32[]{:S(2)}, u32[]{:S(2)}) async-start(bf16[16,16,128]{2,1,0:T(8,128)(2,1)} %shard_map.105), calls=%async_computation.3 | async-start | bytes 131072 | tf_op jit(solution)/shard_map/all_to_all | solution.py:177

commit v6 on v5

--- a/solution.py
+++ b/solution.py
@@ -13,6 +13,7 @@
 BF16 = jnp.bfloat16
 Z_LO = 2
 LINE = ("y", "x")
+PLANE = ("y", "x", "core")
 NEAR = ("y", "x", "z_lo", "core")
 FAR = "z_hi"
 ALL = ("y", "x", "z_hi", "z_lo", "core")
@@ -126,9 +127,20 @@
     return [(first + k) % count for k in range(count)]
 
 
-def from_ahead(value, axis, step):
-    n = lax.axis_size(axis)
-    return lax.ppermute(value, axis, [((i + step) % n, i) for i in range(n)])
+def in_plane(side):
+    return lambda y, x, core: (y % side * side + x % side) * 2 + core
+
+
+def first_lines(side):
+    at, each = in_plane(side), range(side)
+    return [[at(y, x, 0) for x in each] for y in each] + [[at(y, x, 1) for y in each] for x in each]
+
+
+def from_ahead(value, side, step):
+    at, each = in_plane(side), range(side)
+    pairs = [(at(y + step, x, 0), at(y, x, 0)) for y in each for x in each]
+    pairs += [(at(y, x + step, 1), at(y, x, 1)) for y in each for x in each]
+    return lax.ppermute(value, PLANE, pairs)
 
 
 def body(features, adjacency, src_tile, dst_peer, dst_tile, w_self, w_neigh, out_grad):
@@ -140,8 +152,13 @@
     rows = 2 * width * width // near // 128
     peer = dst_peer.reshape(count)
     lead = parts * 10 // 16
-    n_y, n_x = lax.axis_size("y"), lax.axis_size("x")
-    ahead = (peer // n_x - lax.axis_index("y")) % n_y * n_x + peer % n_x
+    side = math.isqrt(parts)
+    peer_y, peer_x = peer // side, peer % side
+    ahead = jnp.where(
+        lax.axis_index("core") == 0,
+        (peer_y - lax.axis_index("y")) % side * side + peer_x,
+        (peer_x - lax.axis_index("x")) % side * side + peer_y,
+    )
     dense = pl.pallas_call(
         functools.partial(partial_sums, lead=lead),
         out_shape=shape((parts, nodes, width), BF16),
@@ -161,7 +178,7 @@
         (
             shape((nodes, width), BF16),
             shape((nodes, width), F32),
-            shape((n_x, nodes, width), BF16),
+            shape((side, nodes, width), BF16),
             shape((near, rows, 128), BF16),
         ),
         0,
@@ -169,17 +186,17 @@
         flops=12 * nodes * width * width,
         size=5 << 20,
     )(recv, features, w_self, w_neigh, out_grad)
-    line = lax.all_to_all(line, "x", 0, 0)
+    line = lax.all_to_all(line, PLANE, 0, 0, axis_index_groups=first_lines(side))
     line, wgrad = lax.optimization_barrier((line, wgrad))
     wgrad = lax.all_to_all(wgrad, NEAR, 0, 0)
-    stacks = [line] + [from_ahead(line, "y", k) for k in range(1, n_y)]
+    stacks = [line] + [from_ahead(line, side, k) for k in range(1, side)]
     wgrad = call(spread_sum, shape((far, rows, 128), BF16), 0, 1, size=1 << 19)(wgrad)
     wgrad = lax.all_to_all(wgrad, FAR, 0, 0, axis_index_groups=[led_by(far * 10 // 16, far)])
     feat_grad = call(
         gradient,
         shape((nodes, width), BF16),
         3,
-        2 + n_y,
+        2 + side,
         scratch=[pltpu.VMEM((nodes, width), F32), pltpu.VMEM((parts, nodes, width), BF16)],
         flops=2 * count * tile * tile * width,
         size=3 << 20,

time: 128 us -> 127 us (level)
    all_to_all x1, starting transfers between devices: 18.3 us -> 16.6 us  [body(): wgrad = lax.all_to_all(wgrad, NEAR, 0, 0)]
where the time goes in v6:
time: 127 us; the launch traced here: 126 us
  starting transfers between devices  54.8 us (43%)
  blocking collectives  53.8 us (42%)
  waiting for transfers between devices  8.85 us (7%)
  Pallas kernels  7.74 us (6%)
    all_to_all x1, starting transfers between devices, body(): lax.all_to_all(wgrad, FAR, 0, 0, axis_index_groups=[led_by(far * 10 // 16...  28.7 us
    all_to_all x1, blocking collectives, body(): lax.all_to_all(dense, LINE, 0, 0, axis_index_groups=[led_by(lead, parts)])  23 us
    all_to_all x1, blocking collectives, body(): wgrad = lax.all_to_all(wgrad, NEAR, 0, 0)  18.3 us
    all_to_all x1, starting transfers between devices, body(): wgrad = lax.all_to_all(wgrad, NEAR, 0, 0)  16.6 us
    all_to_all x1, blocking collectives, body(): lax.all_to_all(line, PLANE, 0, 0, axis_index_groups=first_lines(side))  12.6 us
    ppermute x3, starting transfers between devices, from_ahead(): return lax.ppermute(value, PLANE, pairs)  9.48 us
    all_to_all x1, waiting for transfers between devices, body(): lax.all_to_all(wgrad, FAR, 0, 0, axis_index_groups=[led_by(far * 10 // 16...  8.35 us
    pallas_call x1, Pallas kernels, body(): pl.pallas_call(functools.partial(partial_sums, lead=lead), out_shape=shap...  2.94 us
  transfers between devices with their start and end apart: 5, of which 2 were waited for; matrix products, arithmetic and copies ran while one was open for 0% of the time, Pallas kernels for 2%

profile of v6, /device:TPU:1, one launch (start us, length us, event | category | flops | bytes accessed | tf_op | source)
XLA Modules:
  0.0 126.1 jit_solution(5839444399231454626)
XLA Ops:
  0.6 2.9 %shard_map.103 = bf16[16,256,256]{2,1,0:T(8,128)(2,1)} custom-call(s32[16]{0:T(128)} %src_ref.1, s32[16]{0:T(128)} %bitcast.2, s32[16]{0:T(128)} %dst_ref.1, bf16[256,256]{1,0:T(8,128)(2,1)} %feat_ref.1, bf16[16,128,128]{2,1,0:T(8,128)(2,1)} %adj_ref.1), custom_call_target="tpu_custom_call" | custom-call | flops 134217728 | bytes 3145728 | tf_op jit(solution)/shard_map/pallas_call | solution.py:162
  3.6 0.0 copy-start.1
  3.6 0.0 copy-start.2
  3.6 0.0 copy-start.3
  3.6 0.0 copy-start.4
  3.6 23.0 %all_to_all.25.recv_ref = bf16[16,256,256]{2,1,0:T(8,128)(2,1)S(1)} all-to-all(bf16[16,256,256]{2,1,0:T(8,128)(2,1)} %shard_map.103), channel_id=1, replica_groups={{640,704,768,832,896,960,0,64,128,192,256,320,384,448,512,576},{641,705..., dimensions={0} | all-to-all | bytes 4194304 | tf_op jit(solution)/shard_map/all_to_all | solution.py:175
  26.6 0.0 copy-done.1
  26.6 0.0 copy-done.2
  26.6 0.0 copy-done.3
  26.6 0.0 copy-done.4
  26.6 0.0 copy-start.7
  26.6 0.0 copy-start
  26.6 0.0 copy-start.5
  26.6 0.0 copy-start.6
  26.6 1.4 %shard_map.104 = (bf16[256,256]{1,0:T(8,128)(2,1)}, f32[256,256]{1,0:T(8,128)S(1)}, bf16[4,256,256]{2,1,0:T(8,128)(2,1)S(1)}, bf16[64,16,128]{2,1,0:T(8,128)(2,1)}) custom-call(bf16[16,256,256]{2,1,0:T(8,128)(2,1)S(1)} %all_to_all.25.recv_ref, bf16[256,256]{1,0:T(8,128)(2,1)S(1)} %copy-done.1, bf16[256,256]{1,0:T(8,128)(2,1)S(1)} %copy-done.2, ...), custom_call_target="tpu_custom_call" | custom-call | flops 201326592 | bytes 5242880 | tf_op jit(solution)/shard_map/pallas_call | solution.py:176
  28.1 12.6 %all_to_all.26.s0 = bf16[4,256,256]{2,1,0:T(8,128)(2,1)S(1)} all-to-all(bf16[4,256,256]{2,1,0:T(8,128)(2,1)S(1)} %get-tuple-element.12), channel_id=1, replica_groups={{0,64,128,192},{256,320,384,448},{512,576,640,704},{768,832,896,960},{1..., dimensions={0} | all-to-all | bytes 1048576 | tf_op jit(solution)/shard_map/all_to_all | solution.py:189
  40.6 16.6 %all-to-all-start.2 = ((bf16[64,16,128]{2,1,0:T(8,128)(2,1)}), bf16[64,16,128]{2,1,0:T(8,128)(2,1)S(1)}, u32[]{:S(2)}, u32[]{:S(2)}) async-start(bf16[64,16,128]{2,1,0:T(8,128)(2,1)} %get-tuple-element.14), calls=%async_computation.2 | async-start | bytes 524288 | tf_op jit(solution)/shard_map/all_to_all | solution.py:191
  57.3 4.5 %collective-permute-start = (bf16[4,256,256]{2,1,0:T(8,128)(2,1)S(1)}, bf16[4,256,256]{2,1,0:T(8,128)(2,1)S(1)}, u32[]{:S(2)}, u32[]{:S(2)}) collective-permute-start(bf16[4,256,256]{2,1,0:T(8,128)(2,1)S(1)} %all_to_all.26.s0), channel_id=1, source_target_pairs={{256,0},{320,64},{384,128},{448,192},{512,256},{576,320},{640,384}... | collective-permute-start | bytes 1572872 | tf_op jit(solution)/shard_map/ppermute | solution.py:143
  61.8 2.5 %collective-permute-start.1 = (bf16[4,256,256]{2,1,0:T(8,128)(2,1)S(1)}, bf16[4,256,256]{2,1,0:T(8,128)(2,1)S(1)}, u32[]{:S(2)}, u32[]{:S(2)}) collective-permute-start(bf16[4,256,256]{2,1,0:T(8,128)(2,1)S(1)} %all_to_all.26.s0), channel_id=1, source_target_pairs={{512,0},{576,64},{640,128},{704,192},{768,256},{832,320},{896,384}... | collective-permute-start | bytes 1572872 | tf_op jit(solution)/shard_map/ppermute | solution.py:143
  64.3 2.5 %collective-permute-start.2 = (bf16[4,256,256]{2,1,0:T(8,128)(2,1)S(1)}, bf16[4,256,256]{2,1,0:T(8,128)(2,1)S(1)}, u32[]{:S(2)}, u32[]{:S(2)}) collective-permute-start(bf16[4,256,256]{2,1,0:T(8,128)(2,1)S(1)} %all_to_all.26.s0), channel_id=1, source_target_pairs={{768,0},{832,64},{896,128},{960,192},{0,256},{64,320},{128,384},{1... | collective-permute-start | bytes 1572872 | tf_op jit(solution)/shard_map/ppermute | solution.py:143
  66.8 0.5 all-to-all-done.2.in_ref
  67.3 0.7 shard_map.105
  68.0 28.7 %all-to-all-start.3 = ((bf16[16,16,128]{2,1,0:T(8,128)(2,1)}), bf16[16,16,128]{2,1,0:T(8,128)(2,1)S(1)}, u32[]{:S(2)}, u32[]{:S(2)}) async-start(bf16[16,16,128]{2,1,0:T(8,128)(2,1)} %shard_map.105), calls=%async_computation.3 | async-start | bytes 131072 | tf_op jit(solution)/shard_map/all_to_all | solution.py:194
  96.6 0.0 copy-done.7
  96.7 0.0 collective-permute-done.s1
  96.7 0.0 collective-permute-done.1.s2
  96.7 0.0 collective-permute-done.2.s3
  96.7 0.0 copy-done
  96.7 0.0 copy-done.5
  96.7 0.0 copy-done.6
  96.7 1.8 %shard_map.106 = bf16[256,256]{1,0:T(8,128)(2,1)} custom-call(s32[16]{0:T(128)S(1)} %copy-done.5, s32[16]{0:T(128)S(1)} %broadcast_select_fusion.peer_ref, s32[16]{0:T(128)S(1)} %copy-done.6, bf16[16,128,128]{2,1,0:T(8,128)(2,1)S(1)} %copy-done, f32[256,256]{1,0:T(8,128)S(1)} %get-tuple-element.15.base_ref, bf16[4,256,256]{2,1,0:T(8,128)(2,1)S(1)} %all_to_all.26.s0, ...), custom_call_target="tpu_custom_call" | custom-call | flops 134217728 | bytes 3145728 | tf_op jit(solution)/shard_map/pallas_call | solution.py:195
  98.5 8.4 %all-to-all-done.3.in_ref = bf16[16,16,128]{2,1,0:T(8,128)(2,1)S(1)} async-done(((bf16[16,16,128]{2,1,0:T(8,128)(2,1)}), bf16[16,16,128]{2,1,0:T(8,128)(2,1)S(1)}, u32[]{:S(2)}, u32[]{:S(2)}) %all-to-all-start.3) | async-done | bytes 65568 | tf_op jit(solution)/shard_map/all_to_all | solution.py:194
  106.9 18.3 %all_to_all.27.in_ref = bf16[64,16,128]{2,1,0:T(8,128)(2,1)S(1)} all-to-all(bf16[64,16,128]{2,1,0:T(8,128)(2,1)S(1)} %shard_map.107), channel_id=1, replica_groups=mesh['y'=4,'x'=4,'z_hi'=16,'z_lo'=2,'core'=2] {'y','x','z_lo','core'}, dimensions={0} | all-to-all | bytes 524288 | tf_op jit(solution)/shard_map/all_to_all | solution.py:206
  125.2 0.8 shard_map.108
  (2 shorter events, 0.1 us)
Async XLA Ops:
  3.6 23.0 %copy-start.1 = (bf16[256,256]{1,0:T(8,128)(2,1)S(1)}, bf16[256,256]{1,0:T(8,128)(2,1)}, u32[]{:S(2)}) copy-start(bf16[256,256]{1,0:T(8,128)(2,1)} %feat_ref.1) | copy-start | bytes 393220
  3.6 23.0 %copy-start.2 = (bf16[256,256]{1,0:T(8,128)(2,1)S(1)}, bf16[256,256]{1,0:T(8,128)(2,1)}, u32[]{:S(2)}) copy-start(bf16[256,256]{1,0:T(8,128)(2,1)} %ws_ref.1) | copy-start | bytes 393220
  3.6 23.0 %copy-start.3 = (bf16[256,256]{1,0:T(8,128)(2,1)S(1)}, bf16[256,256]{1,0:T(8,128)(2,1)}, u32[]{:S(2)}) copy-start(bf16[256,256]{1,0:T(8,128)(2,1)} %wn_ref.1) | copy-start | bytes 393220
  3.6 23.0 %copy-start.4 = (bf16[256,256]{1,0:T(8,128)(2,1)S(1)}, bf16[256,256]{1,0:T(8,128)(2,1)}, u32[]{:S(2)}) copy-start(bf16[256,256]{1,0:T(8,128)(2,1)} %grad_ref.1) | copy-start | bytes 393220
  26.6 70.0 %copy-start.7 = (s32[16,1]{0,1:T(1,128)S(1)}, s32[16,1]{0,1:T(1,128)}, u32[]{:S(2)}) copy-start(s32[16,1]{0,1:T(1,128)} %param.11) | copy-start | bytes 196
  26.6 70.1 %copy-start = (bf16[16,128,128]{2,1,0:T(8,128)(2,1)S(1)}, bf16[16,128,128]{2,1,0:T(8,128)(2,1)}, u32[]{:S(2)}) copy-start(bf16[16,128,128]{2,1,0:T(8,128)(2,1)} %adj_ref.1) | copy-start | bytes 1572868
  26.6 70.1 %copy-start.5 = (s32[16]{0:T(128)S(1)}, s32[16]{0:T(128)}, u32[]{:S(2)}) copy-start(s32[16]{0:T(128)} %src_ref.1) | copy-start | bytes 196
  26.6 70.1 %copy-start.6 = (s32[16]{0:T(128)S(1)}, s32[16]{0:T(128)}, u32[]{:S(2)}) copy-start(s32[16]{0:T(128)} %dst_ref.1) | copy-start | bytes 196
  40.6 26.6 %all-to-all-start.2 = ((bf16[64,16,128]{2,1,0:T(8,128)(2,1)}), bf16[64,16,128]{2,1,0:T(8,128)(2,1)S(1)}, u32[]{:S(2)}, u32[]{:S(2)}) async-start(bf16[64,16,128]{2,1,0:T(8,128)(2,1)} %get-tuple-element.14), calls=%async_computation.2 | async-start | bytes 524288 | tf_op jit(solution)/shard_map/all_to_all | solution.py:191
  57.3 39.4 %collective-permute-start = (bf16[4,256,256]{2,1,0:T(8,128)(2,1)S(1)}, bf16[4,256,256]{2,1,0:T(8,128)(2,1)S(1)}, u32[]{:S(2)}, u32[]{:S(2)}) collective-permute-start(bf16[4,256,256]{2,1,0:T(8,128)(2,1)S(1)} %all_to_all.26.s0), channel_id=1, source_target_pairs={{256,0},{320,64},{384,128},{448,192},{512,256},{576,320},{640,384}... | collective-permute-start | bytes 1572872 | tf_op jit(solution)/shard_map/ppermute | solution.py:143
  61.8 34.9 %collective-permute-start.1 = (bf16[4,256,256]{2,1,0:T(8,128)(2,1)S(1)}, bf16[4,256,256]{2,1,0:T(8,128)(2,1)S(1)}, u32[]{:S(2)}, u32[]{:S(2)}) collective-permute-start(bf16[4,256,256]{2,1,0:T(8,128)(2,1)S(1)} %all_to_all.26.s0), channel_id=1, source_target_pairs={{512,0},{576,64},{640,128},{704,192},{768,256},{832,320},{896,384}... | collective-permute-start | bytes 1572872 | tf_op jit(solution)/shard_map/ppermute | solution.py:143
  64.3 32.4 %collective-permute-start.2 = (bf16[4,256,256]{2,1,0:T(8,128)(2,1)S(1)}, bf16[4,256,256]{2,1,0:T(8,128)(2,1)S(1)}, u32[]{:S(2)}, u32[]{:S(2)}) collective-permute-start(bf16[4,256,256]{2,1,0:T(8,128)(2,1)S(1)} %all_to_all.26.s0), channel_id=1, source_target_pairs={{768,0},{832,64},{896,128},{960,192},{0,256},{64,320},{128,384},{1... | collective-permute-start | bytes 1572872 | tf_op jit(solution)/shard_map/ppermute | solution.py:143
  68.0 38.9 %all-to-all-start.3 = ((bf16[16,16,128]{2,1,0:T(8,128)(2,1)}), bf16[16,16,128]{2,1,0:T(8,128)(2,1)S(1)}, u32[]{:S(2)}, u32[]{:S(2)}) async-start(bf16[16,16,128]{2,1,0:T(8,128)(2,1)} %shard_map.105), calls=%async_computation.3 | async-start | bytes 131072 | tf_op jit(solution)/shard_map/all_to_all | solution.py:194

commit v7 on v6

--- a/solution.py
+++ b/solution.py
@@ -188,7 +188,7 @@
     )(recv, features, w_self, w_neigh, out_grad)
     line = lax.all_to_all(line, PLANE, 0, 0, axis_index_groups=first_lines(side))
     line, wgrad = lax.optimization_barrier((line, wgrad))
-    wgrad = lax.all_to_all(wgrad, NEAR, 0, 0)
+    wgrad = lax.all_to_all(wgrad, NEAR, 0, 0, axis_index_groups=[led_by(near * 10 // 16, near)])
     stacks = [line] + [from_ahead(line, side, k) for k in range(1, side)]
     wgrad = call(spread_sum, shape((far, rows, 128), BF16), 0, 1, size=1 << 19)(wgrad)
     wgrad = lax.all_to_all(wgrad, FAR, 0, 0, axis_index_groups=[led_by(far * 10 // 16, far)])
@@ -203,7 +203,7 @@
     )(src_tile, ahead, dst_tile, adjacency, base, *stacks)
     wgrad, feat_grad = lax.optimization_barrier((wgrad, feat_grad))
     wgrad = call(spread_sum, shape((near, rows, 128), BF16), 0, 1, size=1 << 19)(wgrad)
-    wgrad = lax.all_to_all(wgrad, NEAR, 0, 0)
+    wgrad = lax.all_to_all(wgrad, NEAR, 0, 0, axis_index_groups=[led_by(near * 10 // 16, near)])
 
     def last(in_ref, out_ref):
         unpack(in_ref, out_ref, scale=1.0 / math.sqrt(total_nodes))

time: 127 us -> 124 us (0.976)
  waiting for transfers between devices: 8.85 us -> 6.23 us
  starting transfers between devices: 54.8 us -> 56.2 us
  blocking collectives: 53.8 us -> 52.5 us
    all_to_all x1, starting transfers between devices: 16.6 us -> 19.9 us  [body(): lax.all_to_all(wgrad, NEAR, 0, 0, axis_index_groups=[led_by(near * 10 //...]
    ppermute x3, starting transfers between devices: 9.48 us -> 7.23 us  [from_ahead(): return lax.ppermute(value, PLANE, pairs)]
    all_to_all x1, waiting for transfers between devices: 8.35 us -> 6.22 us  [body(): lax.all_to_all(wgrad, FAR, 0, 0, axis_index_groups=[led_by(far * 10 // 16...]
    all_to_all x1, blocking collectives: 18.3 us -> 17 us  [body(): lax.all_to_all(wgrad, NEAR, 0, 0, axis_index_groups=[led_by(near * 10 //...]
  transfers between devices with their start and end apart: 5 -> 5, of which waited for: 2 -> 1; matrix products, arithmetic and copies ran while one was open for 0% -> 0% of each run, Pallas kernels for 2% -> 2%
where the time goes in v7:
time: 124 us; the launch traced here: 123 us
  starting transfers between devices  56.2 us (45%)
  blocking collectives  52.5 us (42%)
  Pallas kernels  7.74 us (6%)
  waiting for transfers between devices  6.23 us (5%)
    all_to_all x1, starting transfers between devices, body(): lax.all_to_all(wgrad, FAR, 0, 0, axis_index_groups=[led_by(far * 10 // 16...  29 us
    all_to_all x1, blocking collectives, body(): lax.all_to_all(dense, LINE, 0, 0, axis_index_groups=[led_by(lead, parts)])  23 us
    all_to_all x1, starting transfers between devices, body(): lax.all_to_all(wgrad, NEAR, 0, 0, axis_index_groups=[led_by(near * 10 //...  19.9 us
    all_to_all x1, blocking collectives, body(): lax.all_to_all(wgrad, NEAR, 0, 0, axis_index_groups=[led_by(near * 10 //...  17 us
    all_to_all x1, blocking collectives, body(): lax.all_to_all(line, PLANE, 0, 0, axis_index_groups=first_lines(side))  12.6 us
    ppermute x3, starting transfers between devices, from_ahead(): return lax.ppermute(value, PLANE, pairs)  7.23 us
    all_to_all x1, waiting for transfers between devices, body(): lax.all_to_all(wgrad, FAR, 0, 0, axis_index_groups=[led_by(far * 10 // 16...  6.22 us
    pallas_call x1, Pallas kernels, body(): pl.pallas_call(functools.partial(partial_sums, lead=lead), out_shape=shap...  2.94 us
  transfers between devices with their start and end apart: 5, of which 1 were waited for; matrix products, arithmetic and copies ran while one was open for 0% of the time, Pallas kernels for 2%

profile of v7, /device:TPU:1, one launch (start us, length us, event | category | flops | bytes accessed | tf_op | source)
XLA Modules:
  0.0 123.5 jit_solution(6696466513371071615)
XLA Ops:
  0.6 2.9 %shard_map.103 = bf16[16,256,256]{2,1,0:T(8,128)(2,1)} custom-call(s32[16]{0:T(128)} %src_ref.1, s32[16]{0:T(128)} %bitcast.2, s32[16]{0:T(128)} %dst_ref.1, bf16[256,256]{1,0:T(8,128)(2,1)} %feat_ref.1, bf16[16,128,128]{2,1,0:T(8,128)(2,1)} %adj_ref.1), custom_call_target="tpu_custom_call" | custom-call | flops 134217728 | bytes 3145728 | tf_op jit(solution)/shard_map/pallas_call | solution.py:162
  3.6 0.0 copy-start.1
  3.6 0.0 copy-start.2
  3.6 0.0 copy-start.3
  3.6 0.0 copy-start.4
  3.6 23.0 %all_to_all.25.recv_ref = bf16[16,256,256]{2,1,0:T(8,128)(2,1)S(1)} all-to-all(bf16[16,256,256]{2,1,0:T(8,128)(2,1)} %shard_map.103), channel_id=1, replica_groups={{640,704,768,832,896,960,0,64,128,192,256,320,384,448,512,576},{641,705..., dimensions={0} | all-to-all | bytes 4194304 | tf_op jit(solution)/shard_map/all_to_all | solution.py:175
  26.6 0.0 copy-done.1
  26.6 0.0 copy-done.2
  26.6 0.0 copy-done.3
  26.6 0.0 copy-done.4
  26.6 0.0 copy-start.7
  26.6 0.0 copy-start
  26.6 0.0 copy-start.5
  26.6 0.0 copy-start.6
  26.6 1.4 %shard_map.104 = (bf16[256,256]{1,0:T(8,128)(2,1)}, f32[256,256]{1,0:T(8,128)S(1)}, bf16[4,256,256]{2,1,0:T(8,128)(2,1)S(1)}, bf16[64,16,128]{2,1,0:T(8,128)(2,1)}) custom-call(bf16[16,256,256]{2,1,0:T(8,128)(2,1)S(1)} %all_to_all.25.recv_ref, bf16[256,256]{1,0:T(8,128)(2,1)S(1)} %copy-done.1, bf16[256,256]{1,0:T(8,128)(2,1)S(1)} %copy-done.2, ...), custom_call_target="tpu_custom_call" | custom-call | flops 201326592 | bytes 5242880 | tf_op jit(solution)/shard_map/pallas_call | solution.py:176
  28.1 12.6 %all_to_all.26.s0 = bf16[4,256,256]{2,1,0:T(8,128)(2,1)S(1)} all-to-all(bf16[4,256,256]{2,1,0:T(8,128)(2,1)S(1)} %get-tuple-element.12), channel_id=1, replica_groups={{0,64,128,192},{256,320,384,448},{512,576,640,704},{768,832,896,960},{1..., dimensions={0} | all-to-all | bytes 1048576 | tf_op jit(solution)/shard_map/all_to_all | solution.py:189
  40.6 19.9 %all-to-all-start.2 = ((bf16[64,16,128]{2,1,0:T(8,128)(2,1)}), bf16[64,16,128]{2,1,0:T(8,128)(2,1)S(1)}, u32[]{:S(2)}, u32[]{:S(2)}) async-start(bf16[64,16,128]{2,1,0:T(8,128)(2,1)} %get-tuple-element.14), calls=%async_computation.2 | async-start | bytes 524288 | tf_op jit(solution)/shard_map/all_to_all | solution.py:191
  60.5 2.3 %collective-permute-start = (bf16[4,256,256]{2,1,0:T(8,128)(2,1)S(1)}, bf16[4,256,256]{2,1,0:T(8,128)(2,1)S(1)}, u32[]{:S(2)}, u32[]{:S(2)}) collective-permute-start(bf16[4,256,256]{2,1,0:T(8,128)(2,1)S(1)} %all_to_all.26.s0), channel_id=1, source_target_pairs={{256,0},{320,64},{384,128},{448,192},{512,256},{576,320},{640,384}... | collective-permute-start | bytes 1572872 | tf_op jit(solution)/shard_map/ppermute | solution.py:143
  62.8 3.0 %collective-permute-start.1 = (bf16[4,256,256]{2,1,0:T(8,128)(2,1)S(1)}, bf16[4,256,256]{2,1,0:T(8,128)(2,1)S(1)}, u32[]{:S(2)}, u32[]{:S(2)}) collective-permute-start(bf16[4,256,256]{2,1,0:T(8,128)(2,1)S(1)} %all_to_all.26.s0), channel_id=1, source_target_pairs={{512,0},{576,64},{640,128},{704,192},{768,256},{832,320},{896,384}... | collective-permute-start | bytes 1572872 | tf_op jit(solution)/shard_map/ppermute | solution.py:143
  65.9 1.9 %collective-permute-start.2 = (bf16[4,256,256]{2,1,0:T(8,128)(2,1)S(1)}, bf16[4,256,256]{2,1,0:T(8,128)(2,1)S(1)}, u32[]{:S(2)}, u32[]{:S(2)}) collective-permute-start(bf16[4,256,256]{2,1,0:T(8,128)(2,1)S(1)} %all_to_all.26.s0), channel_id=1, source_target_pairs={{768,0},{832,64},{896,128},{960,192},{0,256},{64,320},{128,384},{1... | collective-permute-start | bytes 1572872 | tf_op jit(solution)/shard_map/ppermute | solution.py:143
  67.8 0.0 all-to-all-done.2.in_ref
  67.8 0.7 shard_map.105
  68.5 29.0 %all-to-all-start.3 = ((bf16[16,16,128]{2,1,0:T(8,128)(2,1)}), bf16[16,16,128]{2,1,0:T(8,128)(2,1)S(1)}, u32[]{:S(2)}, u32[]{:S(2)}) async-start(bf16[16,16,128]{2,1,0:T(8,128)(2,1)} %shard_map.105), calls=%async_computation.3 | async-start | bytes 131072 | tf_op jit(solution)/shard_map/all_to_all | solution.py:194
  97.5 0.0 copy-done.7
  97.6 0.0 collective-permute-done.s1
  97.6 0.0 collective-permute-done.1.s2
  97.6 0.0 collective-permute-done.2.s3
  97.6 0.0 copy-done
  97.6 0.0 copy-done.5
  97.6 0.0 copy-done.6
  97.6 1.8 %shard_map.106 = bf16[256,256]{1,0:T(8,128)(2,1)} custom-call(s32[16]{0:T(128)S(1)} %copy-done.5, s32[16]{0:T(128)S(1)} %broadcast_select_fusion.peer_ref, s32[16]{0:T(128)S(1)} %copy-done.6, bf16[16,128,128]{2,1,0:T(8,128)(2,1)S(1)} %copy-done, f32[256,256]{1,0:T(8,128)S(1)} %get-tuple-element.15.base_ref, bf16[4,256,256]{2,1,0:T(8,128)(2,1)S(1)} %all_to_all.26.s0, ...), custom_call_target="tpu_custom_call" | custom-call | flops 134217728 | bytes 3145728 | tf_op jit(solution)/shard_map/pallas_call | solution.py:195
  99.4 6.2 %all-to-all-done.3.in_ref = bf16[16,16,128]{2,1,0:T(8,128)(2,1)S(1)} async-done(((bf16[16,16,128]{2,1,0:T(8,128)(2,1)}), bf16[16,16,128]{2,1,0:T(8,128)(2,1)S(1)}, u32[]{:S(2)}, u32[]{:S(2)}) %all-to-all-start.3) | async-done | bytes 65568 | tf_op jit(solution)/shard_map/all_to_all | solution.py:194
  105.7 17.0 %all_to_all.27.in_ref = bf16[64,16,128]{2,1,0:T(8,128)(2,1)S(1)} all-to-all(bf16[64,16,128]{2,1,0:T(8,128)(2,1)S(1)} %shard_map.107), channel_id=1, replica_groups={{640,641,642,643,704,705,706,707,768,769,770,771,832,833,834,835,896,89..., dimensions={0} | all-to-all | bytes 524288 | tf_op jit(solution)/shard_map/all_to_all | solution.py:206
  122.7 0.8 shard_map.108
  (2 shorter events, 0.1 us)
Async XLA Ops:
  3.6 23.0 %copy-start.1 = (bf16[256,256]{1,0:T(8,128)(2,1)S(1)}, bf16[256,256]{1,0:T(8,128)(2,1)}, u32[]{:S(2)}) copy-start(bf16[256,256]{1,0:T(8,128)(2,1)} %feat_ref.1) | copy-start | bytes 393220
  3.6 23.0 %copy-start.2 = (bf16[256,256]{1,0:T(8,128)(2,1)S(1)}, bf16[256,256]{1,0:T(8,128)(2,1)}, u32[]{:S(2)}) copy-start(bf16[256,256]{1,0:T(8,128)(2,1)} %ws_ref.1) | copy-start | bytes 393220
  3.6 23.0 %copy-start.3 = (bf16[256,256]{1,0:T(8,128)(2,1)S(1)}, bf16[256,256]{1,0:T(8,128)(2,1)}, u32[]{:S(2)}) copy-start(bf16[256,256]{1,0:T(8,128)(2,1)} %wn_ref.1) | copy-start | bytes 393220
  3.6 23.0 %copy-start.4 = (bf16[256,256]{1,0:T(8,128)(2,1)S(1)}, bf16[256,256]{1,0:T(8,128)(2,1)}, u32[]{:S(2)}) copy-start(bf16[256,256]{1,0:T(8,128)(2,1)} %grad_ref.1) | copy-start | bytes 393220
  26.6 70.9 %copy-start.7 = (s32[16,1]{0,1:T(1,128)S(1)}, s32[16,1]{0,1:T(1,128)}, u32[]{:S(2)}) copy-start(s32[16,1]{0,1:T(1,128)} %param.11) | copy-start | bytes 196
  26.6 71.0 %copy-start = (bf16[16,128,128]{2,1,0:T(8,128)(2,1)S(1)}, bf16[16,128,128]{2,1,0:T(8,128)(2,1)}, u32[]{:S(2)}) copy-start(bf16[16,128,128]{2,1,0:T(8,128)(2,1)} %adj_ref.1) | copy-start | bytes 1572868
  26.6 71.0 %copy-start.5 = (s32[16]{0:T(128)S(1)}, s32[16]{0:T(128)}, u32[]{:S(2)}) copy-start(s32[16]{0:T(128)} %src_ref.1) | copy-start | bytes 196
  26.6 71.0 %copy-start.6 = (s32[16]{0:T(128)S(1)}, s32[16]{0:T(128)}, u32[]{:S(2)}) copy-start(s32[16]{0:T(128)} %dst_ref.1) | copy-start | bytes 196
  40.6 27.2 %all-to-all-start.2 = ((bf16[64,16,128]{2,1,0:T(8,128)(2,1)}), bf16[64,16,128]{2,1,0:T(8,128)(2,1)S(1)}, u32[]{:S(2)}, u32[]{:S(2)}) async-start(bf16[64,16,128]{2,1,0:T(8,128)(2,1)} %get-tuple-element.14), calls=%async_computation.2 | async-start | bytes 524288 | tf_op jit(solution)/shard_map/all_to_all | solution.py:191
  60.5 37.0 %collective-permute-start = (bf16[4,256,256]{2,1,0:T(8,128)(2,1)S(1)}, bf16[4,256,256]{2,1,0:T(8,128)(2,1)S(1)}, u32[]{:S(2)}, u32[]{:S(2)}) collective-permute-start(bf16[4,256,256]{2,1,0:T(8,128)(2,1)S(1)} %all_to_all.26.s0), channel_id=1, source_target_pairs={{256,0},{320,64},{384,128},{448,192},{512,256},{576,320},{640,384}... | collective-permute-start | bytes 1572872 | tf_op jit(solution)/shard_map/ppermute | solution.py:143
  62.8 34.8 %collective-permute-start.1 = (bf16[4,256,256]{2,1,0:T(8,128)(2,1)S(1)}, bf16[4,256,256]{2,1,0:T(8,128)(2,1)S(1)}, u32[]{:S(2)}, u32[]{:S(2)}) collective-permute-start(bf16[4,256,256]{2,1,0:T(8,128)(2,1)S(1)} %all_to_all.26.s0), channel_id=1, source_target_pairs={{512,0},{576,64},{640,128},{704,192},{768,256},{832,320},{896,384}... | collective-permute-start | bytes 1572872 | tf_op jit(solution)/shard_map/ppermute | solution.py:143
  65.9 31.7 %collective-permute-start.2 = (bf16[4,256,256]{2,1,0:T(8,128)(2,1)S(1)}, bf16[4,256,256]{2,1,0:T(8,128)(2,1)S(1)}, u32[]{:S(2)}, u32[]{:S(2)}) collective-permute-start(bf16[4,256,256]{2,1,0:T(8,128)(2,1)S(1)} %all_to_all.26.s0), channel_id=1, source_target_pairs={{768,0},{832,64},{896,128},{960,192},{0,256},{64,320},{128,384},{1... | collective-permute-start | bytes 1572872 | tf_op jit(solution)/shard_map/ppermute | solution.py:143
  68.5 37.1 %all-to-all-start.3 = ((bf16[16,16,128]{2,1,0:T(8,128)(2,1)}), bf16[16,16,128]{2,1,0:T(8,128)(2,1)S(1)}, u32[]{:S(2)}, u32[]{:S(2)}) async-start(bf16[16,16,128]{2,1,0:T(8,128)(2,1)} %shard_map.105), calls=%async_computation.3 | async-start | bytes 131072 | tf_op jit(solution)/shard_map/all_to_all | solution.py:194

commit v8 on v7

--- a/solution.py
+++ b/solution.py
@@ -132,8 +132,8 @@
 
 
 def first_lines(side):
-    at, each = in_plane(side), range(side)
-    return [[at(y, x, 0) for x in each] for y in each] + [[at(y, x, 1) for y in each] for x in each]
+    at, each, led = in_plane(side), range(side), led_by(side // 2, side)
+    return [[at(y, x, 0) for x in led] for y in each] + [[at(y, x, 1) for y in led] for x in each]
 
 
 def from_ahead(value, side, step):
@@ -156,8 +156,8 @@
     peer_y, peer_x = peer // side, peer % side
     ahead = jnp.where(
         lax.axis_index("core") == 0,
-        (peer_y - lax.axis_index("y")) % side * side + peer_x,
-        (peer_x - lax.axis_index("x")) % side * side + peer_y,
+        (peer_y - lax.axis_index("y")) % side * side + (peer_x - side // 2) % side,
+        (peer_x - lax.axis_index("x")) % side * side + (peer_y - side // 2) % side,
     )
     dense = pl.pallas_call(
         functools.partial(partial_sums, lead=lead),

time: 124 us -> 123 us (level)
  no operation moved by 1% of the time
where the time goes in v8:
time: 123 us; the launch traced here: 122 us
  starting transfers between devices  55.1 us (45%)
  blocking collectives  52.3 us (43%)
  Pallas kernels  7.74 us (6%)
  waiting for transfers between devices  6.23 us (5%)
    all_to_all x1, starting transfers between devices, body(): lax.all_to_all(wgrad, FAR, 0, 0, axis_index_groups=[led_by(far * 10 // 16...  27.9 us
    all_to_all x1, blocking collectives, body(): lax.all_to_all(dense, LINE, 0, 0, axis_index_groups=[led_by(lead, parts)])  23 us
    all_to_all x1, starting transfers between devices, body(): lax.all_to_all(wgrad, NEAR, 0, 0, axis_index_groups=[led_by(near * 10 //...  19.9 us
    all_to_all x1, blocking collectives, body(): lax.all_to_all(wgrad, NEAR, 0, 0, axis_index_groups=[led_by(near * 10 //...  17 us
    all_to_all x1, blocking collectives, body(): lax.all_to_all(line, PLANE, 0, 0, axis_index_groups=first_lines(side))  12.4 us
    ppermute x3, starting transfers between devices, from_ahead(): return lax.ppermute(value, PLANE, pairs)  7.23 us
    all_to_all x1, waiting for transfers between devices, body(): lax.all_to_all(wgrad, FAR, 0, 0, axis_index_groups=[led_by(far * 10 // 16...  6.22 us
    pallas_call x1, Pallas kernels, body(): pl.pallas_call(functools.partial(partial_sums, lead=lead), out_shape=shap...  2.94 us
  transfers between devices with their start and end apart: 5, of which 1 were waited for; matrix products, arithmetic and copies ran while one was open for 0% of the time, Pallas kernels for 2%

profile of v8, /device:TPU:1, one launch (start us, length us, event | category | flops | bytes accessed | tf_op | source)
XLA Modules:
  0.0 122.2 jit_solution(9841522691908723194)
XLA Ops:
  0.6 2.9 %shard_map.103 = bf16[16,256,256]{2,1,0:T(8,128)(2,1)} custom-call(s32[16]{0:T(128)} %src_ref.1, s32[16]{0:T(128)} %bitcast.2, s32[16]{0:T(128)} %dst_ref.1, bf16[256,256]{1,0:T(8,128)(2,1)} %feat_ref.1, bf16[16,128,128]{2,1,0:T(8,128)(2,1)} %adj_ref.1), custom_call_target="tpu_custom_call" | custom-call | flops 134217728 | bytes 3145728 | tf_op jit(solution)/shard_map/pallas_call | solution.py:162
  3.6 0.0 copy-start.1
  3.6 0.0 copy-start.2
  3.6 0.0 copy-start.3
  3.6 0.0 copy-start.4
  3.6 23.0 %all_to_all.25.recv_ref = bf16[16,256,256]{2,1,0:T(8,128)(2,1)S(1)} all-to-all(bf16[16,256,256]{2,1,0:T(8,128)(2,1)} %shard_map.103), channel_id=1, replica_groups={{640,704,768,832,896,960,0,64,128,192,256,320,384,448,512,576},{641,705..., dimensions={0} | all-to-all | bytes 4194304 | tf_op jit(solution)/shard_map/all_to_all | solution.py:175
  26.6 0.0 copy-done.1
  26.6 0.0 copy-done.2
  26.6 0.0 copy-done.3
  26.6 0.0 copy-done.4
  26.6 0.0 copy-start.7
  26.6 0.0 copy-start
  26.6 0.0 copy-start.5
  26.6 0.0 copy-start.6
  26.6 1.4 %shard_map.104 = (bf16[256,256]{1,0:T(8,128)(2,1)}, f32[256,256]{1,0:T(8,128)S(1)}, bf16[4,256,256]{2,1,0:T(8,128)(2,1)S(1)}, bf16[64,16,128]{2,1,0:T(8,128)(2,1)}) custom-call(bf16[16,256,256]{2,1,0:T(8,128)(2,1)S(1)} %all_to_all.25.recv_ref, bf16[256,256]{1,0:T(8,128)(2,1)S(1)} %copy-done.1, bf16[256,256]{1,0:T(8,128)(2,1)S(1)} %copy-done.2, ...), custom_call_target="tpu_custom_call" | custom-call | flops 201326592 | bytes 5242880 | tf_op jit(solution)/shard_map/pallas_call | solution.py:176
  28.1 12.4 %all_to_all.26.s0 = bf16[4,256,256]{2,1,0:T(8,128)(2,1)S(1)} all-to-all(bf16[4,256,256]{2,1,0:T(8,128)(2,1)S(1)} %get-tuple-element.12), channel_id=1, replica_groups={{128,192,0,64},{384,448,256,320},{640,704,512,576},{896,960,768,832},{5..., dimensions={0} | all-to-all | bytes 1048576 | tf_op jit(solution)/shard_map/all_to_all | solution.py:189
  40.4 19.9 %all-to-all-start.2 = ((bf16[64,16,128]{2,1,0:T(8,128)(2,1)}), bf16[64,16,128]{2,1,0:T(8,128)(2,1)S(1)}, u32[]{:S(2)}, u32[]{:S(2)}) async-start(bf16[64,16,128]{2,1,0:T(8,128)(2,1)} %get-tuple-element.14), calls=%async_computation.2 | async-start | bytes 524288 | tf_op jit(solution)/shard_map/all_to_all | solution.py:191
  60.3 2.3 %collective-permute-start = (bf16[4,256,256]{2,1,0:T(8,128)(2,1)S(1)}, bf16[4,256,256]{2,1,0:T(8,128)(2,1)S(1)}, u32[]{:S(2)}, u32[]{:S(2)}) collective-permute-start(bf16[4,256,256]{2,1,0:T(8,128)(2,1)S(1)} %all_to_all.26.s0), channel_id=1, source_target_pairs={{256,0},{320,64},{384,128},{448,192},{512,256},{576,320},{640,384}... | collective-permute-start | bytes 1572872 | tf_op jit(solution)/shard_map/ppermute | solution.py:143
  62.6 3.0 %collective-permute-start.1 = (bf16[4,256,256]{2,1,0:T(8,128)(2,1)S(1)}, bf16[4,256,256]{2,1,0:T(8,128)(2,1)S(1)}, u32[]{:S(2)}, u32[]{:S(2)}) collective-permute-start(bf16[4,256,256]{2,1,0:T(8,128)(2,1)S(1)} %all_to_all.26.s0), channel_id=1, source_target_pairs={{512,0},{576,64},{640,128},{704,192},{768,256},{832,320},{896,384}... | collective-permute-start | bytes 1572872 | tf_op jit(solution)/shard_map/ppermute | solution.py:143
  65.7 1.9 %collective-permute-start.2 = (bf16[4,256,256]{2,1,0:T(8,128)(2,1)S(1)}, bf16[4,256,256]{2,1,0:T(8,128)(2,1)S(1)}, u32[]{:S(2)}, u32[]{:S(2)}) collective-permute-start(bf16[4,256,256]{2,1,0:T(8,128)(2,1)S(1)} %all_to_all.26.s0), channel_id=1, source_target_pairs={{768,0},{832,64},{896,128},{960,192},{0,256},{64,320},{128,384},{1... | collective-permute-start | bytes 1572872 | tf_op jit(solution)/shard_map/ppermute | solution.py:143
  67.6 0.0 all-to-all-done.2.in_ref
  67.6 0.7 shard_map.105
  68.3 27.9 %all-to-all-start.3 = ((bf16[16,16,128]{2,1,0:T(8,128)(2,1)}), bf16[16,16,128]{2,1,0:T(8,128)(2,1)S(1)}, u32[]{:S(2)}, u32[]{:S(2)}) async-start(bf16[16,16,128]{2,1,0:T(8,128)(2,1)} %shard_map.105), calls=%async_computation.3 | async-start | bytes 131072 | tf_op jit(solution)/shard_map/all_to_all | solution.py:194
  96.2 0.0 copy-done.7
  96.3 0.0 collective-permute-done.s1
  96.3 0.0 collective-permute-done.1.s2
  96.3 0.0 collective-permute-done.2.s3
  96.3 0.0 copy-done
  96.3 0.0 copy-done.5
  96.3 0.0 copy-done.6
  96.3 1.8 %shard_map.106 = bf16[256,256]{1,0:T(8,128)(2,1)} custom-call(s32[16]{0:T(128)S(1)} %copy-done.5, s32[16]{0:T(128)S(1)} %broadcast_select_fusion.peer_ref, s32[16]{0:T(128)S(1)} %copy-done.6, bf16[16,128,128]{2,1,0:T(8,128)(2,1)S(1)} %copy-done, f32[256,256]{1,0:T(8,128)S(1)} %get-tuple-element.15.base_ref, bf16[4,256,256]{2,1,0:T(8,128)(2,1)S(1)} %all_to_all.26.s0, ...), custom_call_target="tpu_custom_call" | custom-call | flops 134217728 | bytes 3145728 | tf_op jit(solution)/shard_map/pallas_call | solution.py:195
  98.2 6.2 %all-to-all-done.3.in_ref = bf16[16,16,128]{2,1,0:T(8,128)(2,1)S(1)} async-done(((bf16[16,16,128]{2,1,0:T(8,128)(2,1)}), bf16[16,16,128]{2,1,0:T(8,128)(2,1)S(1)}, u32[]{:S(2)}, u32[]{:S(2)}) %all-to-all-start.3) | async-done | bytes 65568 | tf_op jit(solution)/shard_map/all_to_all | solution.py:194
  104.4 17.0 %all_to_all.27.in_ref = bf16[64,16,128]{2,1,0:T(8,128)(2,1)S(1)} all-to-all(bf16[64,16,128]{2,1,0:T(8,128)(2,1)S(1)} %shard_map.107), channel_id=1, replica_groups={{640,641,642,643,704,705,706,707,768,769,770,771,832,833,834,835,896,89..., dimensions={0} | all-to-all | bytes 524288 | tf_op jit(solution)/shard_map/all_to_all | solution.py:206
  121.4 0.8 shard_map.108
  (2 shorter events, 0.1 us)
Async XLA Ops:
  3.6 23.0 %copy-start.1 = (bf16[256,256]{1,0:T(8,128)(2,1)S(1)}, bf16[256,256]{1,0:T(8,128)(2,1)}, u32[]{:S(2)}) copy-start(bf16[256,256]{1,0:T(8,128)(2,1)} %feat_ref.1) | copy-start | bytes 393220
  3.6 23.0 %copy-start.2 = (bf16[256,256]{1,0:T(8,128)(2,1)S(1)}, bf16[256,256]{1,0:T(8,128)(2,1)}, u32[]{:S(2)}) copy-start(bf16[256,256]{1,0:T(8,128)(2,1)} %ws_ref.1) | copy-start | bytes 393220
  3.6 23.0 %copy-start.3 = (bf16[256,256]{1,0:T(8,128)(2,1)S(1)}, bf16[256,256]{1,0:T(8,128)(2,1)}, u32[]{:S(2)}) copy-start(bf16[256,256]{1,0:T(8,128)(2,1)} %wn_ref.1) | copy-start | bytes 393220
  3.6 23.0 %copy-start.4 = (bf16[256,256]{1,0:T(8,128)(2,1)S(1)}, bf16[256,256]{1,0:T(8,128)(2,1)}, u32[]{:S(2)}) copy-start(bf16[256,256]{1,0:T(8,128)(2,1)} %grad_ref.1) | copy-start | bytes 393220
  26.6 69.7 %copy-start.7 = (s32[16,1]{0,1:T(1,128)S(1)}, s32[16,1]{0,1:T(1,128)}, u32[]{:S(2)}) copy-start(s32[16,1]{0,1:T(1,128)} %param.11) | copy-start | bytes 196
  26.6 69.7 %copy-start = (bf16[16,128,128]{2,1,0:T(8,128)(2,1)S(1)}, bf16[16,128,128]{2,1,0:T(8,128)(2,1)}, u32[]{:S(2)}) copy-start(bf16[16,128,128]{2,1,0:T(8,128)(2,1)} %adj_ref.1) | copy-start | bytes 1572868
  26.6 69.7 %copy-start.5 = (s32[16]{0:T(128)S(1)}, s32[16]{0:T(128)}, u32[]{:S(2)}) copy-start(s32[16]{0:T(128)} %src_ref.1) | copy-start | bytes 196
  26.6 69.7 %copy-start.6 = (s32[16]{0:T(128)S(1)}, s32[16]{0:T(128)}, u32[]{:S(2)}) copy-start(s32[16]{0:T(128)} %dst_ref.1) | copy-start | bytes 196
  40.4 27.1 %all-to-all-start.2 = ((bf16[64,16,128]{2,1,0:T(8,128)(2,1)}), bf16[64,16,128]{2,1,0:T(8,128)(2,1)S(1)}, u32[]{:S(2)}, u32[]{:S(2)}) async-start(bf16[64,16,128]{2,1,0:T(8,128)(2,1)} %get-tuple-element.14), calls=%async_computation.2 | async-start | bytes 524288 | tf_op jit(solution)/shard_map/all_to_all | solution.py:191
  60.3 35.9 %collective-permute-start = (bf16[4,256,256]{2,1,0:T(8,128)(2,1)S(1)}, bf16[4,256,256]{2,1,0:T(8,128)(2,1)S(1)}, u32[]{:S(2)}, u32[]{:S(2)}) collective-permute-start(bf16[4,256,256]{2,1,0:T(8,128)(2,1)S(1)} %all_to_all.26.s0), channel_id=1, source_target_pairs={{256,0},{320,64},{384,128},{448,192},{512,256},{576,320},{640,384}... | collective-permute-start | bytes 1572872 | tf_op jit(solution)/shard_map/ppermute | solution.py:143
  62.6 33.7 %collective-permute-start.1 = (bf16[4,256,256]{2,1,0:T(8,128)(2,1)S(1)}, bf16[4,256,256]{2,1,0:T(8,128)(2,1)S(1)}, u32[]{:S(2)}, u32[]{:S(2)}) collective-permute-start(bf16[4,256,256]{2,1,0:T(8,128)(2,1)S(1)} %all_to_all.26.s0), channel_id=1, source_target_pairs={{512,0},{576,64},{640,128},{704,192},{768,256},{832,320},{896,384}... | collective-permute-start | bytes 1572872 | tf_op jit(solution)/shard_map/ppermute | solution.py:143
  65.7 30.6 %collective-permute-start.2 = (bf16[4,256,256]{2,1,0:T(8,128)(2,1)S(1)}, bf16[4,256,256]{2,1,0:T(8,128)(2,1)S(1)}, u32[]{:S(2)}, u32[]{:S(2)}) collective-permute-start(bf16[4,256,256]{2,1,0:T(8,128)(2,1)S(1)} %all_to_all.26.s0), channel_id=1, source_target_pairs={{768,0},{832,64},{896,128},{960,192},{0,256},{64,320},{128,384},{1... | collective-permute-start | bytes 1572872 | tf_op jit(solution)/shard_map/ppermute | solution.py:143
  68.3 36.1 %all-to-all-start.3 = ((bf16[16,16,128]{2,1,0:T(8,128)(2,1)}), bf16[16,16,128]{2,1,0:T(8,128)(2,1)S(1)}, u32[]{:S(2)}, u32[]{:S(2)}) async-start(bf16[16,16,128]{2,1,0:T(8,128)(2,1)} %shard_map.105), calls=%async_computation.3 | async-start | bytes 131072 | tf_op jit(solution)/shard_map/all_to_all | solution.py:194

commit v9 on v8

--- a/solution.py
+++ b/solution.py
@@ -188,7 +188,7 @@
     )(recv, features, w_self, w_neigh, out_grad)
     line = lax.all_to_all(line, PLANE, 0, 0, axis_index_groups=first_lines(side))
     line, wgrad = lax.optimization_barrier((line, wgrad))
-    wgrad = lax.all_to_all(wgrad, NEAR, 0, 0, axis_index_groups=[led_by(near * 10 // 16, near)])
+    wgrad = lax.all_to_all(wgrad, NEAR, 0, 0, axis_index_groups=[led_by(near * 11 // 16, near)])
     stacks = [line] + [from_ahead(line, side, k) for k in range(1, side)]
     wgrad = call(spread_sum, shape((far, rows, 128), BF16), 0, 1, size=1 << 19)(wgrad)
     wgrad = lax.all_to_all(wgrad, FAR, 0, 0, axis_index_groups=[led_by(far * 10 // 16, far)])
@@ -203,7 +203,7 @@
     )(src_tile, ahead, dst_tile, adjacency, base, *stacks)
     wgrad, feat_grad = lax.optimization_barrier((wgrad, feat_grad))
     wgrad = call(spread_sum, shape((near, rows, 128), BF16), 0, 1, size=1 << 19)(wgrad)
-    wgrad = lax.all_to_all(wgrad, NEAR, 0, 0, axis_index_groups=[led_by(near * 10 // 16, near)])
+    wgrad = lax.all_to_all(wgrad, NEAR, 0, 0, axis_index_groups=[led_by(near * 11 // 16, near)])
 
     def last(in_ref, out_ref):
         unpack(in_ref, out_ref, scale=1.0 / math.sqrt(total_nodes))

time: 123 us -> 124 us (level)
  waiting for transfers between devices: 6.23 us -> 7.9 us
    all_to_all x1, waiting for transfers between devices: 6.22 us -> 7.89 us  [body(): lax.all_to_all(wgrad, FAR, 0, 0, axis_index_groups=[led_by(far * 10 // 16...]
where the time goes in v9:
time: 124 us; the launch traced here: 123 us
  starting transfers between devices  55.8 us (45%)
  blocking collectives  51.1 us (41%)
  waiting for transfers between devices  7.9 us (6%)
  Pallas kernels  7.74 us (6%)
    all_to_all x1, starting transfers between devices, body(): lax.all_to_all(wgrad, FAR, 0, 0, axis_index_groups=[led_by(far * 10 // 16...  28.4 us
    all_to_all x1, blocking collectives, body(): lax.all_to_all(dense, LINE, 0, 0, axis_index_groups=[led_by(lead, parts)])  23 us
    all_to_all x1, starting transfers between devices, body(): lax.all_to_all(wgrad, NEAR, 0, 0, axis_index_groups=[led_by(near * 11 //...  19.3 us
    all_to_all x1, blocking collectives, body(): lax.all_to_all(wgrad, NEAR, 0, 0, axis_index_groups=[led_by(near * 11 //...  15.8 us
    all_to_all x1, blocking collectives, body(): lax.all_to_all(line, PLANE, 0, 0, axis_index_groups=first_lines(side))  12.4 us
    ppermute x3, starting transfers between devices, from_ahead(): return lax.ppermute(value, PLANE, pairs)  8.13 us
    all_to_all x1, waiting for transfers between devices, body(): lax.all_to_all(wgrad, FAR, 0, 0, axis_index_groups=[led_by(far * 10 // 16...  7.89 us
    pallas_call x1, Pallas kernels, body(): pl.pallas_call(functools.partial(partial_sums, lead=lead), out_shape=shap...  2.94 us
  transfers between devices with their start and end apart: 5, of which 1 were waited for; matrix products, arithmetic and copies ran while one was open for 0% of the time, Pallas kernels for 2%

profile of v9, /device:TPU:1, one launch (start us, length us, event | category | flops | bytes accessed | tf_op | source)
XLA Modules:
  0.0 123.4 jit_solution(2160914962550676112)
XLA Ops:
  0.6 2.9 %shard_map.103 = bf16[16,256,256]{2,1,0:T(8,128)(2,1)} custom-call(s32[16]{0:T(128)} %src_ref.1, s32[16]{0:T(128)} %bitcast.2, s32[16]{0:T(128)} %dst_ref.1, bf16[256,256]{1,0:T(8,128)(2,1)} %feat_ref.1, bf16[16,128,128]{2,1,0:T(8,128)(2,1)} %adj_ref.1), custom_call_target="tpu_custom_call" | custom-call | flops 134217728 | bytes 3145728 | tf_op jit(solution)/shard_map/pallas_call | solution.py:162
  3.6 0.0 copy-start.1
  3.6 0.0 copy-start.2
  3.6 0.0 copy-start.3
  3.6 0.0 copy-start.4
  3.6 23.0 %all_to_all.25.recv_ref = bf16[16,256,256]{2,1,0:T(8,128)(2,1)S(1)} all-to-all(bf16[16,256,256]{2,1,0:T(8,128)(2,1)} %shard_map.103), channel_id=1, replica_groups={{640,704,768,832,896,960,0,64,128,192,256,320,384,448,512,576},{641,705..., dimensions={0} | all-to-all | bytes 4194304 | tf_op jit(solution)/shard_map/all_to_all | solution.py:175
  26.6 0.0 copy-done.1
  26.6 0.0 copy-done.2
  26.6 0.0 copy-done.3
  26.6 0.0 copy-done.4
  26.6 0.0 copy-start.7
  26.6 0.0 copy-start
  26.6 0.0 copy-start.5
  26.6 0.0 copy-start.6
  26.6 1.4 %shard_map.104 = (bf16[256,256]{1,0:T(8,128)(2,1)}, f32[256,256]{1,0:T(8,128)S(1)}, bf16[4,256,256]{2,1,0:T(8,128)(2,1)S(1)}, bf16[64,16,128]{2,1,0:T(8,128)(2,1)}) custom-call(bf16[16,256,256]{2,1,0:T(8,128)(2,1)S(1)} %all_to_all.25.recv_ref, bf16[256,256]{1,0:T(8,128)(2,1)S(1)} %copy-done.1, bf16[256,256]{1,0:T(8,128)(2,1)S(1)} %copy-done.2, ...), custom_call_target="tpu_custom_call" | custom-call | flops 201326592 | bytes 5242880 | tf_op jit(solution)/shard_map/pallas_call | solution.py:176
  28.1 12.4 %all_to_all.26.s0 = bf16[4,256,256]{2,1,0:T(8,128)(2,1)S(1)} all-to-all(bf16[4,256,256]{2,1,0:T(8,128)(2,1)S(1)} %get-tuple-element.12), channel_id=1, replica_groups={{128,192,0,64},{384,448,256,320},{640,704,512,576},{896,960,768,832},{5..., dimensions={0} | all-to-all | bytes 1048576 | tf_op jit(solution)/shard_map/all_to_all | solution.py:189
  40.4 19.3 %all-to-all-start.2 = ((bf16[64,16,128]{2,1,0:T(8,128)(2,1)}), bf16[64,16,128]{2,1,0:T(8,128)(2,1)S(1)}, u32[]{:S(2)}, u32[]{:S(2)}) async-start(bf16[64,16,128]{2,1,0:T(8,128)(2,1)} %get-tuple-element.14), calls=%async_computation.2 | async-start | bytes 524288 | tf_op jit(solution)/shard_map/all_to_all | solution.py:191
  59.8 2.3 %collective-permute-start = (bf16[4,256,256]{2,1,0:T(8,128)(2,1)S(1)}, bf16[4,256,256]{2,1,0:T(8,128)(2,1)S(1)}, u32[]{:S(2)}, u32[]{:S(2)}) collective-permute-start(bf16[4,256,256]{2,1,0:T(8,128)(2,1)S(1)} %all_to_all.26.s0), channel_id=1, source_target_pairs={{256,0},{320,64},{384,128},{448,192},{512,256},{576,320},{640,384}... | collective-permute-start | bytes 1572872 | tf_op jit(solution)/shard_map/ppermute | solution.py:143
  62.0 3.9 %collective-permute-start.1 = (bf16[4,256,256]{2,1,0:T(8,128)(2,1)S(1)}, bf16[4,256,256]{2,1,0:T(8,128)(2,1)S(1)}, u32[]{:S(2)}, u32[]{:S(2)}) collective-permute-start(bf16[4,256,256]{2,1,0:T(8,128)(2,1)S(1)} %all_to_all.26.s0), channel_id=1, source_target_pairs={{512,0},{576,64},{640,128},{704,192},{768,256},{832,320},{896,384}... | collective-permute-start | bytes 1572872 | tf_op jit(solution)/shard_map/ppermute | solution.py:143
  66.0 1.9 %collective-permute-start.2 = (bf16[4,256,256]{2,1,0:T(8,128)(2,1)S(1)}, bf16[4,256,256]{2,1,0:T(8,128)(2,1)S(1)}, u32[]{:S(2)}, u32[]{:S(2)}) collective-permute-start(bf16[4,256,256]{2,1,0:T(8,128)(2,1)S(1)} %all_to_all.26.s0), channel_id=1, source_target_pairs={{768,0},{832,64},{896,128},{960,192},{0,256},{64,320},{128,384},{1... | collective-permute-start | bytes 1572872 | tf_op jit(solution)/shard_map/ppermute | solution.py:143
  67.9 0.0 all-to-all-done.2.in_ref
  67.9 0.7 shard_map.105
  68.6 28.4 %all-to-all-start.3 = ((bf16[16,16,128]{2,1,0:T(8,128)(2,1)}), bf16[16,16,128]{2,1,0:T(8,128)(2,1)S(1)}, u32[]{:S(2)}, u32[]{:S(2)}) async-start(bf16[16,16,128]{2,1,0:T(8,128)(2,1)} %shard_map.105), calls=%async_computation.3 | async-start | bytes 131072 | tf_op jit(solution)/shard_map/all_to_all | solution.py:194
  97.0 0.0 copy-done.7
  97.0 0.0 collective-permute-done.s1
  97.1 0.0 collective-permute-done.1.s2
  97.1 0.0 collective-permute-done.2.s3
  97.1 0.0 copy-done
  97.1 0.0 copy-done.5
  97.1 0.0 copy-done.6
  97.1 1.8 %shard_map.106 = bf16[256,256]{1,0:T(8,128)(2,1)} custom-call(s32[16]{0:T(128)S(1)} %copy-done.5, s32[16]{0:T(128)S(1)} %broadcast_select_fusion.peer_ref, s32[16]{0:T(128)S(1)} %copy-done.6, bf16[16,128,128]{2,1,0:T(8,128)(2,1)S(1)} %copy-done, f32[256,256]{1,0:T(8,128)S(1)} %get-tuple-element.15.base_ref, bf16[4,256,256]{2,1,0:T(8,128)(2,1)S(1)} %all_to_all.26.s0, ...), custom_call_target="tpu_custom_call" | custom-call | flops 134217728 | bytes 3145728 | tf_op jit(solution)/shard_map/pallas_call | solution.py:195
  98.9 7.9 %all-to-all-done.3.in_ref = bf16[16,16,128]{2,1,0:T(8,128)(2,1)S(1)} async-done(((bf16[16,16,128]{2,1,0:T(8,128)(2,1)}), bf16[16,16,128]{2,1,0:T(8,128)(2,1)S(1)}, u32[]{:S(2)}, u32[]{:S(2)}) %all-to-all-start.3) | async-done | bytes 65568 | tf_op jit(solution)/shard_map/all_to_all | solution.py:194
  106.9 15.8 %all_to_all.27.in_ref = bf16[64,16,128]{2,1,0:T(8,128)(2,1)S(1)} all-to-all(bf16[64,16,128]{2,1,0:T(8,128)(2,1)S(1)} %shard_map.107), channel_id=1, replica_groups={{704,705,706,707,768,769,770,771,832,833,834,835,896,897,898,899,960,96..., dimensions={0} | all-to-all | bytes 524288 | tf_op jit(solution)/shard_map/all_to_all | solution.py:206
  122.6 0.8 shard_map.108
  (2 shorter events, 0.1 us)
Async XLA Ops:
  3.6 23.0 %copy-start.1 = (bf16[256,256]{1,0:T(8,128)(2,1)S(1)}, bf16[256,256]{1,0:T(8,128)(2,1)}, u32[]{:S(2)}) copy-start(bf16[256,256]{1,0:T(8,128)(2,1)} %feat_ref.1) | copy-start | bytes 393220
  3.6 23.0 %copy-start.2 = (bf16[256,256]{1,0:T(8,128)(2,1)S(1)}, bf16[256,256]{1,0:T(8,128)(2,1)}, u32[]{:S(2)}) copy-start(bf16[256,256]{1,0:T(8,128)(2,1)} %ws_ref.1) | copy-start | bytes 393220
  3.6 23.0 %copy-start.3 = (bf16[256,256]{1,0:T(8,128)(2,1)S(1)}, bf16[256,256]{1,0:T(8,128)(2,1)}, u32[]{:S(2)}) copy-start(bf16[256,256]{1,0:T(8,128)(2,1)} %wn_ref.1) | copy-start | bytes 393220
  3.6 23.0 %copy-start.4 = (bf16[256,256]{1,0:T(8,128)(2,1)S(1)}, bf16[256,256]{1,0:T(8,128)(2,1)}, u32[]{:S(2)}) copy-start(bf16[256,256]{1,0:T(8,128)(2,1)} %grad_ref.1) | copy-start | bytes 393220
  26.6 70.4 %copy-start.7 = (s32[16,1]{0,1:T(1,128)S(1)}, s32[16,1]{0,1:T(1,128)}, u32[]{:S(2)}) copy-start(s32[16,1]{0,1:T(1,128)} %param.11) | copy-start | bytes 196
  26.6 70.5 %copy-start = (bf16[16,128,128]{2,1,0:T(8,128)(2,1)S(1)}, bf16[16,128,128]{2,1,0:T(8,128)(2,1)}, u32[]{:S(2)}) copy-start(bf16[16,128,128]{2,1,0:T(8,128)(2,1)} %adj_ref.1) | copy-start | bytes 1572868
  26.6 70.5 %copy-start.5 = (s32[16]{0:T(128)S(1)}, s32[16]{0:T(128)}, u32[]{:S(2)}) copy-start(s32[16]{0:T(128)} %src_ref.1) | copy-start | bytes 196
  26.6 70.5 %copy-start.6 = (s32[16]{0:T(128)S(1)}, s32[16]{0:T(128)}, u32[]{:S(2)}) copy-start(s32[16]{0:T(128)} %dst_ref.1) | copy-start | bytes 196
  40.4 27.5 %all-to-all-start.2 = ((bf16[64,16,128]{2,1,0:T(8,128)(2,1)}), bf16[64,16,128]{2,1,0:T(8,128)(2,1)S(1)}, u32[]{:S(2)}, u32[]{:S(2)}) async-start(bf16[64,16,128]{2,1,0:T(8,128)(2,1)} %get-tuple-element.14), calls=%async_computation.2 | async-start | bytes 524288 | tf_op jit(solution)/shard_map/all_to_all | solution.py:191
  59.8 37.3 %collective-permute-start = (bf16[4,256,256]{2,1,0:T(8,128)(2,1)S(1)}, bf16[4,256,256]{2,1,0:T(8,128)(2,1)S(1)}, u32[]{:S(2)}, u32[]{:S(2)}) collective-permute-start(bf16[4,256,256]{2,1,0:T(8,128)(2,1)S(1)} %all_to_all.26.s0), channel_id=1, source_target_pairs={{256,0},{320,64},{384,128},{448,192},{512,256},{576,320},{640,384}... | collective-permute-start | bytes 1572872 | tf_op jit(solution)/shard_map/ppermute | solution.py:143
  62.0 35.0 %collective-permute-start.1 = (bf16[4,256,256]{2,1,0:T(8,128)(2,1)S(1)}, bf16[4,256,256]{2,1,0:T(8,128)(2,1)S(1)}, u32[]{:S(2)}, u32[]{:S(2)}) collective-permute-start(bf16[4,256,256]{2,1,0:T(8,128)(2,1)S(1)} %all_to_all.26.s0), channel_id=1, source_target_pairs={{512,0},{576,64},{640,128},{704,192},{768,256},{832,320},{896,384}... | collective-permute-start | bytes 1572872 | tf_op jit(solution)/shard_map/ppermute | solution.py:143
  66.0 31.1 %collective-permute-start.2 = (bf16[4,256,256]{2,1,0:T(8,128)(2,1)S(1)}, bf16[4,256,256]{2,1,0:T(8,128)(2,1)S(1)}, u32[]{:S(2)}, u32[]{:S(2)}) collective-permute-start(bf16[4,256,256]{2,1,0:T(8,128)(2,1)S(1)} %all_to_all.26.s0), channel_id=1, source_target_pairs={{768,0},{832,64},{896,128},{960,192},{0,256},{64,320},{128,384},{1... | collective-permute-start | bytes 1572872 | tf_op jit(solution)/shard_map/ppermute | solution.py:143
  68.6 38.2 %all-to-all-start.3 = ((bf16[16,16,128]{2,1,0:T(8,128)(2,1)}), bf16[16,16,128]{2,1,0:T(8,128)(2,1)S(1)}, u32[]{:S(2)}, u32[]{:S(2)}) async-start(bf16[16,16,128]{2,1,0:T(8,128)(2,1)} %shard_map.105), calls=%async_computation.3 | async-start | bytes 131072 | tf_op jit(solution)/shard_map/all_to_all | solution.py:194
